TPU v7x, 32 devices: a whole 2x2x4 slice. The times are simulated.
32 devices in a mesh: surf: 8 (over y, x, core), wall: 4 (over z).
Axes of the slice: x: 2, y: 2, z: 4, core: 2. Of those that a mesh axis runs over, the one named last changes fastest.
Arguments:
- flow_state: float32 [5, 128, 64, 512], P(None, 'wall', 'surf'), may hold values from -1 to 6, as said below
- spacing: float32 [128, 64, 512], P('wall', 'surf'), may hold values from 0.6 to 1.8
- bc_kind: int32 [64, 512], P('surf'), may hold values from 0 to 2
- cell_of: int32 [32768], P(('surf', 'wall')), may hold values from 0 to 32767, as said below
- zone_id: int32 [32768], P(('surf', 'wall')), may hold values from 0 to 7
- abl_temp: float32 [64, 32768], P(None, ('surf', 'wall')), may hold values from 0.5 to 2
- conduct: float32 [8], replicated, may hold values from 0.3 to 3
- diffuse: float32 [8], replicated, may hold values from 0.1 to 0.45
- rate: float32 [8], replicated, may hold values from 0.3 to 3
Outputs:
- state_next: float32 [5, 128, 64, 512], P(None, 'wall', 'surf')
- node_shift: float32 [128, 64, 512], P('wall', 'surf')
- ablator_next: float32 [64, 32768], P(None, ('surf', 'wall'))
Inputs may be any that keep to these rules, and one draw needn't show every extreme that they name: `cell_of`: each surface cell is named by exactly one column; the columns of one device name exactly 128 cells of every surface tile (tile = cell // 4096). `flow_state`: the density U0 is at least 0.45 and the pressure derived from U is at least 0.37 in every cell.
All inputs are finite; a program needn't handle non-finite values.
Results may differ from a plain program's by a relative error of at most 0.0003.
Values sent between devices are 32-bit elements; how exact they have to be, the bound alone decides.
A program may use at most 128 MiB of HBM per device.

v0:
```python
import jax
import jax.numpy as jnp
from jax import lax
from jax.sharding import PartitionSpec as P

heat_ratio = 1.4
time_step = 0.15
viscosity = 0.05
conduction = 0.07
sponge_rate = 0.5
activation = 2.0
blow_ratio = 1.0
radiation = 0.8
film_conduct = 1.0
recovery = 0.2
far_values = (1.0, 0.5, 0.0, 0.0, 2.625)


def from_root(value, axis, source):
    kept = jnp.where(lax.axis_index(axis) == source, value, 0).astype(value.dtype)
    return lax.psum(kept, axis)


def prefix(value, axis, join, neutral):
    count, mine = (lax.axis_size(axis), lax.axis_index(axis))
    pieces = lax.all_gather(value, axis)
    running = jnp.full_like(value, 0) + jnp.asarray(neutral, value.dtype)

    def hop(position, running):
        longer = join(running, pieces[position])
        return jnp.where(position < mine, longer, running)

    return lax.fori_loop(0, count - 1, hop, running)


def padded_2(value, sides, width, wrap):
    for axis, dim in sides:
        size, length = (lax.axis_size(axis), value.shape[dim])
        up = [(i, (i + 1) % size) for i in range(size if wrap else size - 1)]
        down = [(j, i) for i, j in up]
        last = lax.slice_in_dim(value, length - width, length, axis=dim)
        initial = lax.slice_in_dim(value, 0, width, axis=dim)
        before = lax.ppermute(last, axis, up)
        after = lax.ppermute(initial, axis, down)
        value = jnp.concatenate([before, value, after], axis=dim)
    return value


def primitives(values):
    density = values[0]
    velo_x = values[1] / density
    velo_y = values[2] / density
    velo_z = values[3] / density
    kinetic = 0.5 * density * (velo_x * velo_x + velo_y * velo_y + velo_z * velo_z)
    pressure = (heat_ratio - 1.0) * (values[4] - kinetic)
    return (density, velo_x, velo_y, velo_z, pressure)


def conserved(density, velo_x, velo_y, velo_z, pressure):
    energy = pressure / (heat_ratio - 1.0) + 0.5 * density * (
        velo_x * velo_x + velo_y * velo_y + velo_z * velo_z
    )
    return jnp.stack([density, density * velo_x, density * velo_y, density * velo_z, energy])


def wall_ghost(cell_row, surf_temp, surf_blow, kind_rows):
    density, velo_x, velo_y, velo_z, pressure = primitives(cell_row)
    wall_density = pressure / surf_temp
    noslip = conserved(wall_density, -velo_x, -velo_y, -velo_z, pressure)
    slip_state = conserved(density, velo_x, velo_y, -velo_z, pressure)
    blow_state = conserved(wall_density, -velo_x, -velo_y, 2.0 * surf_blow - velo_z, pressure)
    return jnp.where(kind_rows == 0, noslip, jnp.where(kind_rows == 1, slip_state, blow_state))


def shifted_slice(padded, along_axis, offset, length):
    return lax.slice_in_dim(padded, 2 + offset, 2 + offset + length, axis=along_axis)


def first_diff(padded, along_axis, length):
    near_diff = shifted_slice(padded, along_axis, 1, length) - shifted_slice(
        padded, along_axis, -1, length
    )
    outer_diff = shifted_slice(padded, along_axis, 2, length) - shifted_slice(
        padded, along_axis, -2, length
    )
    return (8.0 * near_diff - outer_diff) / 12.0


def second_diff(padded, along_axis, length):
    near_sum = shifted_slice(padded, along_axis, 1, length) + shifted_slice(
        padded, along_axis, -1, length
    )
    outer_sum = shifted_slice(padded, along_axis, 2, length) + shifted_slice(
        padded, along_axis, -2, length
    )
    return (
        16.0 * near_sum - outer_sum - 30.0 * shifted_slice(padded, along_axis, 0, length)
    ) / 12.0


def wrap_last(values):
    return jnp.concatenate([values[..., -2:], values, values[..., :2]], axis=-1)


def fluxes(values, normal):
    density, velo_x, velo_y, velo_z, pressure = primitives(values)
    speeds = (velo_x, velo_y, velo_z)
    normal_speed = speeds[normal]
    momentum_flux = [values[1] * normal_speed, values[2] * normal_speed, values[3] * normal_speed]
    momentum_flux[normal] = momentum_flux[normal] + pressure
    face_flux = jnp.stack(
        [
            values[normal + 1],
            momentum_flux[0],
            momentum_flux[1],
            momentum_flux[2],
            (values[4] + pressure) * normal_speed,
        ]
    )
    lap_fields = jnp.stack([velo_x, velo_y, velo_z, pressure / density])
    return (face_flux, lap_fields)


def advance(padded_state, padded_heights, normalized):
    depth_k = padded_heights.shape[0] - 4
    rows_i = padded_state.shape[2] - 4
    cols_j = padded_state.shape[3]
    center_state = padded_state[:, 2:-2, 2:-2, :]
    side_state = padded_state[:, 2:-2, :, :]
    stack_state = padded_state[:, :, 2:-2, :]
    flux_i, lap_i = fluxes(side_state, 0)
    flux_j, lap_j = fluxes(wrap_last(center_state), 1)
    flux_k, lap_k = fluxes(stack_state, 2)
    metric = first_diff(padded_heights, 0, depth_k)
    convect = (
        first_diff(flux_i, 2, rows_i)
        + first_diff(flux_j, 3, cols_j)
        + first_diff(flux_k, 1, depth_k) / metric
    )
    laplace = (
        second_diff(lap_i, 2, rows_i)
        + second_diff(lap_j, 3, cols_j)
        + second_diff(lap_k, 1, depth_k) / (metric * metric)
    )
    viscous = jnp.stack(
        [
            jnp.zeros_like(laplace[0]),
            viscosity * laplace[0],
            viscosity * laplace[1],
            viscosity * laplace[2],
            conduction * laplace[3],
        ]
    )
    far_field = jnp.array(far_values, jnp.float32)[:, None, None, None]
    sponge = sponge_rate * normalized * normalized * (center_state - far_field)
    return center_state + time_step * (viscous - convect - sponge)


def ablate(abl_temp, col_film, col_recovery, col_conduct, col_diffuse, col_rate):
    inner_temp = abl_temp[1]
    surface = abl_temp[0]
    for newton_pass in range(2):
        surface_cube = surface * surface * surface
        surface = (
            col_film * col_recovery
            + col_conduct * inner_temp
            + 3.0 * radiation * surface_cube * surface
        ) / (col_film + col_conduct + 4.0 * radiation * surface_cube)
    recession = col_rate * jnp.exp(-activation / surface)
    blowing = blow_ratio * recession
    profile = jnp.concatenate([surface[None], abl_temp[1:]], axis=0)
    for heat_pass in range(2):
        middle = profile[1:-1] + col_diffuse * (profile[2:] - 2.0 * profile[1:-1] + profile[:-2])
        bottom = profile[-1] + 2.0 * col_diffuse * (profile[-2] - profile[-1])
        profile = jnp.concatenate([profile[:1], middle, bottom[None]], axis=0)
    return (surface, blowing, recession, profile)


def add_terms(earlier, later):
    return earlier + later


def shards(flow_state, spacing, bc_kind, cell_of, zone_id, abl_temp, conduct, diffuse, rate):
    tile_count = lax.axis_size("surf")
    wall_count = lax.axis_size("wall")
    wall_pos = lax.axis_index("wall")
    rows_i = flow_state.shape[2]
    cols_j = flow_state.shape[3]
    tile_cells = rows_i * cols_j
    density, velo_x, velo_y, velo_z, pressure = primitives(flow_state[:, 0])
    recovery_temp = pressure / density + recovery * (
        velo_x * velo_x + velo_y * velo_y + velo_z * velo_z
    )
    film = film_conduct / (0.5 * spacing[0])
    wall_fields = from_root(jnp.stack([film, recovery_temp]).reshape(2, tile_cells), "wall", 0)
    per_tile = cell_of.shape[0] // tile_count
    owner_tile = cell_of // tile_cells
    within_tile = cell_of % tile_cells
    sort_order = jnp.argsort(owner_tile, stable=True)
    inverse_order = jnp.argsort(sort_order)
    sorted_cells = within_tile[sort_order].reshape(tile_count, per_tile)
    asked_cells = lax.all_to_all(sorted_cells, "surf", split_axis=0, concat_axis=0, tiled=True)
    film_ask = jnp.take(wall_fields[0], asked_cells)
    recovery_ask = jnp.take(wall_fields[1], asked_cells)
    film_back = lax.all_to_all(film_ask, "surf", split_axis=0, concat_axis=0, tiled=True)
    recovery_back = lax.all_to_all(recovery_ask, "surf", split_axis=0, concat_axis=0, tiled=True)
    film_rows, recovery_rows, asked_cells = (film_back, recovery_back, asked_cells)
    col_film = film_rows.reshape(-1)[inverse_order]
    col_recovery = recovery_rows.reshape(-1)[inverse_order]
    zone_mask = (zone_id[None, :] == jnp.arange(conduct.shape[0], dtype=jnp.int32)[:, None]).astype(
        jnp.float32
    )
    col_conduct = jnp.sum(zone_mask * conduct[:, None], axis=0)
    col_diffuse = jnp.sum(zone_mask * diffuse[:, None], axis=0)
    col_rate = jnp.sum(zone_mask * rate[:, None], axis=0)
    surface, blowing, recession, ablator_next = ablate(
        abl_temp, col_film, col_recovery, col_conduct, col_diffuse, col_rate
    )
    outgoing = jnp.stack([surface, blowing, recession])[:, sort_order].reshape(
        3, tile_count, per_tile
    )
    arrived = lax.all_to_all(outgoing, "surf", split_axis=1, concat_axis=1, tiled=True)
    dense_rows = jnp.zeros((3, tile_cells), jnp.float32).at[:, asked_cells].set(arrived)
    slab_total = jnp.sum(spacing, axis=0)
    wall_sums, column_total = lax.psum((dense_rows, slab_total), "wall")
    slab_offset = prefix(slab_total, "wall", add_terms, jnp.zeros_like(slab_total))
    wall_grid = wall_sums.reshape(3, rows_i, cols_j)
    surf_temp = wall_grid[0]
    surf_blow = wall_grid[1]
    surf_recess = wall_grid[2]
    center = slab_offset + jnp.cumsum(spacing, axis=0) - 0.5 * spacing
    node_shift = surf_recess * (center / column_total - 1.0)
    shifted = center + node_shift
    is_bottom = wall_pos == 0
    is_top = wall_pos == wall_count - 1
    padded_state = padded_2(flow_state, (("surf", 2), ("wall", 1)), 2, True)
    padded_heights = padded_2(shifted, (("wall", 0),), 2, False)
    wall_low = jnp.stack([3.0 * shifted[0] - 2.0 * shifted[1], 2.0 * shifted[0] - shifted[1]])
    wall_high = jnp.stack([2.0 * shifted[-1] - shifted[-2], 3.0 * shifted[-1] - 2.0 * shifted[-2]])
    padded_heights = jnp.concatenate(
        [
            jnp.where(is_bottom, wall_low, padded_heights[:2]),
            padded_heights[2:-2],
            jnp.where(is_top, wall_high, padded_heights[-2:]),
        ],
        axis=0,
    )
    ghost_one = wall_ghost(flow_state[:, 0], surf_temp, surf_blow, bc_kind)
    ghost_two = wall_ghost(flow_state[:, 1], surf_temp, surf_blow, bc_kind)
    bottom_rows = jnp.stack([ghost_two, ghost_one], axis=1)
    top_rows = jnp.broadcast_to(
        jnp.array(far_values, jnp.float32)[:, None, None, None], (5, 2, rows_i, cols_j)
    )
    inner_cols = padded_state[:, :, 2:-2, :]
    low_rows = jnp.where(is_bottom, bottom_rows, inner_cols[:, :2])
    high_rows = jnp.where(is_top, top_rows, inner_cols[:, -2:])
    inner_cols = jnp.concatenate([low_rows, inner_cols[:, 2:-2], high_rows], axis=1)
    padded_state = padded_state.at[:, :, 2:-2, :].set(inner_cols)
    state_next = advance(padded_state, padded_heights, center / column_total)
    return (state_next, node_shift, ablator_next)


def solution(mesh):
    in_specs = (
        P(None, "wall", "surf", None),
        P("wall", "surf", None),
        P("surf", None),
        P(("surf", "wall")),
        P(("surf", "wall")),
        P(None, ("surf", "wall")),
        P(),
        P(),
        P(),
    )
    out_specs = (P(None, "wall", "surf", None), P("wall", "surf", None), P(None, ("surf", "wall")))
    return jax.shard_map(shards, mesh=mesh, in_specs=in_specs, out_specs=out_specs, check_vma=False)
```

profile of v0, /device:TPU:0, one launch (start us, length us, event | category | flops | bytes accessed | tf_op | source)
XLA Modules:
  0.0 355.3 jit_solution(15694828613417540038)
XLA Ops:
  8.0 4.4 %sort.34 = (s32[1024]{0:T(1024)}, s32[1024]{0:T(1024)S(1)}) sort(s32[1024]{0:T(1024)S(1)} %get-tuple-element.223, s32[1024]{0:T(1024)S(1)} %iota.12), dimensions={0}, to_apply=%region_0.1 | sort | flops 10240 | bytes 16384 | tf_op jit(solution)/shard_map/jit(argsort)/sort | solution.py:199
  12.4 8.8 %gather_fusion = s32[1024]{0:T(1024)} fusion(s32[1024]{0:T(1024)S(1)} %get-tuple-element.224, s32[1024]{0:T(1024)S(1)} %fusion.49), kind=kCustom, calls=%fused_computation.2 | custom fusion | bytes 12288 | tf_op jit(solution)/shard_map/gather | solution.py:201
  21.2 5.2 %all-to-all-start = ((s32[8,1,128]{2,1,0:T(1,128)}), s32[8,1,128]{2,1,0:T(1,128)S(1)}, u32[]{:S(2)}, u32[]{:S(2)}) async-start(s32[8,1,128]{2,1,0:T(1,128)} %bitcast), calls=%async_computation | async-start | bytes 8192 | tf_op jit(solution)/shard_map/all_to_all | solution.py:202
  26.4 1.5 fusion.61
  28.4 2.2 collective-permute-start.1
  30.6 1.3 fusion.60
  33.2 19.3 %psum.21 = f32[2,4096]{1,0:T(2,128)S(1)} all-reduce(f32[2,4096]{1,0:T(2,128)S(1)} %maximum_select_fusion), channel_id=1, replica_groups=mesh['surf'=8,'wall'=4] {'wall'}, use_global_device_ids=true, to_apply=%region_1.2 | all-reduce | flops 8192 | bytes 65536 | tf_op jit(solution)/shard_map/psum | solution.py:21
  52.5 4.4 %sort.35 = (s32[1024]{0:T(1024)}, s32[1024]{0:T(1024)S(1)}) sort(s32[1024]{0:T(1024)S(1)} %get-tuple-element.97, s32[1024]{0:T(1024)S(1)} %iota.13), dimensions={0}, to_apply=%region_2.4 | sort | flops 10240 | bytes 16384 | tf_op jit(solution)/shard_map/jit(argsort)/sort | solution.py:200
  57.5 13.3 %all-gather = f32[32,512]{1,0:T(8,128)S(1)} all-gather(f32[8,512]{1,0:T(8,128)S(1)} %reduce_sum.44), channel_id=2, replica_groups=mesh['surf'=8,'wall'=4] {'wall'}, dimensions={0}, use_global_device_ids=true | all-gather | bytes 81920 | tf_op jit(solution)/shard_map/all_gather | solution.py:26
  70.9 1.3 broadcast_compare_fusion.1
  72.2 2.4 pad_maximum_fusion.2
  76.5 1.1 add_dynamic-update-slice_fusion.1
  81.4 1.8 pad_maximum_fusion.4
  83.8 10.5 %gather_fusion.5 = f32[1024]{0:T(1024)} fusion(f32[4096]{0:T(1024)S(1)} %bitcast.64, s32[1024]{0:T(1024)S(1)} %bitcast_clamp_fusion), kind=kCustom, calls=%fused_computation.1.clone | custom fusion | bytes 12288 | tf_op jit(solution)/shard_map/jit(_take)/gather | solution.py:204
  94.4 1.3 bitcast_select_fusion
  95.7 6.4 %gather_fusion.4 = f32[1024]{0:T(1024)S(1)} fusion(f32[4096]{0:T(1024)S(1)} %bitcast.63, s32[1024]{0:T(1024)} %copy-done.24), kind=kCustom, calls=%fused_computation.clone | custom fusion | bytes 12288 | tf_op jit(solution)/shard_map/jit(_take)/gather | solution.py:203
  102.7 3.3 all-to-all-start.1
  107.6 3.0 all-to-all-done.1
  110.6 3.3 all-to-all-start.2
  114.5 8.8 %gather_fusion.1 = f32[1024]{0:T(1024)} fusion(f32[1024]{0:T(1024)S(1)} %bitcast.61, s32[1024]{0:T(1024)S(1)} %copy-done.23), kind=kCustom, calls=%fused_computation.3 | custom fusion | bytes 12288 | tf_op jit(solution)/shard_map/gather | solution.py:208
  123.3 8.9 %gather_fusion.2 = f32[1024]{0:T(1024)} fusion(f32[1024]{0:T(1024)S(1)} %bitcast.62, s32[1024]{0:T(1024)S(1)} %copy-done.23), kind=kCustom, calls=%fused_computation.4 | custom fusion | bytes 12288 | tf_op jit(solution)/shard_map/gather | solution.py:209
  134.0 5.1 %gather_fusion.3 = f32[1024,3]{1,0:T(8,128)} fusion(f32[3,1024]{0,1:T(8,128)} %copy.44, s32[1024]{0:T(1024)S(1)} %copy-done.22), kind=kCustom, calls=%fused_computation.5 | custom fusion | bytes 28672 | tf_op jit(solution)/shard_map/gather | solution.py:219
  139.1 1.8 copy.45
  140.9 4.1 %all-to-all-start.3 = ((f32[3,8,128]{2,0,1:T(4,128)}), f32[3,8,128]{2,0,1:T(4,128)S(1)}, u32[]{:S(2)}, u32[]{:S(2)}) async-start(f32[3,8,128]{2,0,1:T(4,128)} %copy.45), calls=%async_computation.3 | async-start | bytes 32768 | tf_op jit(solution)/shard_map/all_to_all | solution.py:222
  147.0 2.8 all-to-all-done.3
  150.8 4.9 %scatter_custom_fusion = f32[3,4096]{0,1:T(8,128)} fusion(s32[1024]{0:T(1024)} %fusion.50, f32[1024,3]{1,0:T(8,128)} %copy.46, f32[]{:T(128)} %constant.146.clone.1), kind=kCustom, calls=%fused_computation.67 | custom fusion | bytes 49664 | tf_op jit(solution)/shard_map/scatter | solution.py:223
  156.5 83.6 %all-reduce.3.cloned.1.call-done = (f32[3,4096]{0,1:T(8,128)}, f32[8,512]{1,0:T(8,128)}) async-done(((f32[3,4096]{0,1:T(8,128)}, f32[8,512]{1,0:T(8,128)}), (f32[3,4096]{0,1:T(8,128)}, f32[8,512]{1,0:T(8,128)})) %all-reduce.3.cloned.1.call-update) | async-done | bytes 65552 | tf_op jit(solution)/shard_map/psum | solution.py:225
  240.1 5.7 %slice_reduce_fusion = (f32[4096]{0:T(1024)S(1)}, f32[4096]{0:T(1024)S(1)}, f32[4096]{0:T(1024)S(1)}) fusion(f32[3,4096]{0,1:T(8,128)} %get-tuple-element.129), kind=kLoop, calls=%fused_computation.35 | loop fusion | flops 4096 | bytes 98304 | tf_op jit(solution)/shard_map/slice | solution.py:230
  245.8 1.2 fusion.59
  247.8 1.3 collective-permute-start.4
  249.1 4.5 %collective-permute-start.5 = (f32[2,8,512]{2,1,0:T(8,128)S(1)}, f32[2,8,512]{2,1,0:T(8,128)S(1)}, u32[]{:S(2)}, u32[]{:S(2)}) collective-permute-start(f32[2,8,512]{2,1,0:T(8,128)S(1)} %get-tuple-element.214), channel_id=1, source_target_pairs={{0,1},{1,2},{2,3},{4,5},{5,6},{6,7},{8,9},{9,10},{10,11},{12,13},{... | collective-permute-start | bytes 98312 | tf_op jit(solution)/shard_map/ppermute | solution.py:43
  256.5 2.7 collective-permute-start.3
  260.3 7.1 %collective-permute-done.3 = f32[5,2,12,512]{3,2,1,0:T(8,128)S(1)} collective-permute-done((f32[5,2,12,512]{3,2,1,0:T(8,128)S(1)}, f32[5,2,12,512]{3,2,1,0:T(8,128)S(1)}, u32[]{:S(2)}, u32[]{:S(2)}) %collective-permute-start.3) | collective-permute-done | bytes 245792 | tf_op jit(solution)/shard_map/ppermute | solution.py:44
  267.5 5.6 %collective-permute-done.2 = f32[5,2,12,512]{3,2,1,0:T(8,128)S(1)} collective-permute-done((f32[5,2,12,512]{3,2,1,0:T(8,128)S(1)}, f32[5,2,12,512]{3,2,1,0:T(8,128)S(1)}, u32[]{:S(2)}, u32[]{:S(2)}) %collective-permute-start.2) | collective-permute-done | bytes 245792 | tf_op jit(solution)/shard_map/ppermute | solution.py:43
  273.6 1.6 copy-done.2
  276.1 4.3 %pad_maximum_fusion = f32[5,36,12,512]{3,2,1,0:T(8,128)} fusion(f32[5,2,12,512]{3,2,1,0:T(8,128)S(1)} %collective-permute-done.3, f32[5,32,2,512]{3,2,1,0:T(2,128)} %collective-permute-done.1, f32[5,32,8,512]{3,2,1,0:T(8,128)S(1)} %copy-done, f32[5,32,2,512]{3,2,1,0:T(2,128)} %collective-permute-done, f32[5,2,12,512]{3,2,1,0:T(8,128)S(1)} %collective-permute-done.2), kind=kLoop, calls=%fused_computation.8 | loop fusion | flops 4423680 | bytes 8847360 | tf_op jit(solution)/shard_map/concatenate | solution.py:45
  280.3 20.4 %scatter.13 = f32[5,36,12,512]{3,2,1,0:T(8,128)} dynamic-update-slice(f32[5,36,12,512]{3,2,1,0:T(8,128)} %pad_maximum_fusion, f32[5,36,8,512]{3,2,1,0:T(8,128)} %copy-done.2, s32[]{:T(128)} %constant.148.clone.1, s32[]{:T(128)} %constant.148.clone.1, s32[]{:T(128)} %constant.164.clone.1, s32[]{:T(128)} %constant.148.clone.1) | dynamic-update-slice | bytes 5898244 | tf_op jit(solution)/shard_map/scatter | solution.py:258
  300.7 1.5 slice_dynamic-update-slice_fusion
  302.2 3.4 add_dynamic-update-slice_fusion
  306.2 1.3 copy-done.3
  310.0 2.9 pad_maximum_fusion.1
  313.6 1.5 copy-done.1
  315.1 10.5 %fusion.16 = f32[4,32,8,512]{3,2,1,0:T(8,128)} fusion(f32[4,36,8,512]{3,2,1,0:T(8,128)S(1)} %pad_maximum_fusion.5, f32[4,32,8,516]{3,2,1,0:T(8,128)S(1)} %copy-done.1, f32[4,32,12,512]{3,2,1,0:T(8,128)} %pad_maximum_fusion.1, f32[32,8,512]{2,1,0:T(8,128)} %get-tuple-element.150), kind=kLoop, calls=%fused_computation.40 | loop fusion | flops 12058624 | bytes 34078720 | tf_op jit(solution)/shard_map/add | solution.py:141
  325.6 1.9 fusion.40
  327.5 1.9 fusion.39
  329.4 1.9 fusion.38
  331.3 1.9 fusion.37
  333.2 15.3 %multiply_add_fusion = f32[5,32,8,512]{3,2,1,0:T(8,128)} fusion(f32[5,32,8,512]{3,2,1,0:T(8,128)S(1)} %copy-done, f32[5,32,8,512]{3,2,1,0:T(8,128)} %fusion.37, f32[5,36,8,512]{3,2,1,0:T(8,128)S(1)} %get-tuple-element.186, f32[5,32,8,516]{3,2,1,0:T(8,128)} %get-tuple-element.182, f32[5,32,12,512]{3,2,1,0:T(8,128)} %copy-done.5, f32[5]{0:T(128)S(1)} %copy-done.32, ...), kind=kLoop, calls=%fused_computation.33 | loop fusion | flops 15073280 | bytes 40370196 | tf_op jit(solution)/shard_map/add | solution.py:156
  (159 shorter events, 27.6 us)
Async XLA Ops:
  7.2 19.2 %copy-start = (f32[5,32,8,512]{3,2,1,0:T(8,128)S(1)}, f32[5,32,8,512]{3,2,1,0:T(8,128)}, u32[]{:S(2)}) copy-start(f32[5,32,8,512]{3,2,1,0:T(8,128)} %param.17) | copy-start | bytes 7864324
  12.4 15.5 %copy-start.21 = (s32[1024]{0:T(1024)}, s32[1024]{0:T(1024)S(1)}, u32[]{:S(2)}) copy-start(s32[1024]{0:T(1024)S(1)} %fusion.49) | copy-start | bytes 12292
  21.2 62.0 %all-to-all-start = ((s32[8,1,128]{2,1,0:T(1,128)}), s32[8,1,128]{2,1,0:T(1,128)S(1)}, u32[]{:S(2)}, u32[]{:S(2)}) async-start(s32[8,1,128]{2,1,0:T(1,128)} %bitcast), calls=%async_computation | async-start | bytes 8192 | tf_op jit(solution)/shard_map/all_to_all | solution.py:202
  26.4 6.3 %copy-start.6 = (f32[32,8,512]{2,1,0:T(8,128)S(1)}, f32[32,8,512]{2,1,0:T(8,128)}, u32[]{:S(2)}) copy-start(f32[32,8,512]{2,1,0:T(8,128)} %param.18) | copy-start | bytes 1572868
  27.9 227.6 %collective-permute-start = (f32[5,32,2,512]{3,2,1,0:T(2,128)}, f32[5,32,2,512]{3,2,1,0:T(2,128)}, u32[]{:S(2)}, u32[]{:S(2)}) collective-permute-start(f32[5,32,2,512]{3,2,1,0:T(2,128)} %get-tuple-element.206), channel_id=1, source_target_pairs={{0,4},{4,8},{8,12},{12,16},{16,20},{20,24},{24,28},{28,0},{1,5},{5... | collective-permute-start | bytes 1966088 | tf_op jit(solution)/shard_map/ppermute | solution.py:43
  28.4 227.1 %collective-permute-start.1 = (f32[5,32,2,512]{3,2,1,0:T(2,128)}, f32[5,32,2,512]{3,2,1,0:T(2,128)}, u32[]{:S(2)}, u32[]{:S(2)}) collective-permute-start(f32[5,32,2,512]{3,2,1,0:T(2,128)} %get-tuple-element.207), channel_id=1, source_target_pairs={{4,0},{8,4},{12,8},{16,12},{20,16},{24,20},{28,24},{0,28},{5,1},{9... | collective-permute-start | bytes 1966088 | tf_op jit(solution)/shard_map/ppermute | solution.py:44
  32.5 0.6 copy-start.13
  57.5 13.4 %copy-start.10 = (f32[8,512]{1,0:T(8,128)}, f32[8,512]{1,0:T(8,128)S(1)}, u32[]{:S(2)}) copy-start(f32[8,512]{1,0:T(8,128)S(1)} %reduce_sum.44) | copy-start | bytes 49156
  76.5 2.1 copy-start.27
  76.5 2.1 copy-start.29
  76.5 2.1 copy-start.30
  76.5 2.1 copy-start.31
  79.2 4.0 %copy-start.17 = (f32[1024]{0:T(1024)}, f32[1024]{0:T(1024)S(1)}, u32[]{:S(2)}) copy-start(f32[1024]{0:T(1024)S(1)} %get-tuple-element.118) | copy-start | bytes 12292
  81.4 1.8 copy-start.15
  83.2 0.6 copy-start.19
  83.2 0.6 copy-start.24
  94.4 12.5 %copy-start.9 = (f32[64,1024]{1,0:T(8,128)S(1)}, f32[64,1024]{1,0:T(8,128)}, u32[]{:S(2)}) copy-start(f32[64,1024]{1,0:T(8,128)} %param.22) | copy-start | bytes 786436
  95.7 18.2 %copy-start.20 = (s32[8,1,128]{2,1,0:T(1,128)S(1)}, s32[8,1,128]{2,1,0:T(1,128)}, u32[]{:S(2)}) copy-start(s32[8,1,128]{2,1,0:T(1,128)} %copy-done.19) | copy-start | bytes 12292
  95.7 18.8 %copy-start.23 = (s32[1024]{0:T(1024)S(1)}, s32[1024]{0:T(1024)}, u32[]{:S(2)}) copy-start(s32[1024]{0:T(1024)} %fusion.51) | copy-start | bytes 12292
  102.7 7.9 %all-to-all-start.1 = ((f32[8,1,128]{2,1,0:T(1,128)}), f32[8,1,128]{2,1,0:T(1,128)S(1)}, u32[]{:S(2)}, u32[]{:S(2)}) async-start(f32[8,1,128]{2,1,0:T(1,128)} %bitcast.8), calls=%async_computation.1 | async-start | bytes 8192 | tf_op jit(solution)/shard_map/all_to_all | solution.py:205
  110.6 12.8 %all-to-all-start.2 = ((f32[8,1,128]{2,1,0:T(1,128)}), f32[8,1,128]{2,1,0:T(1,128)S(1)}, u32[]{:S(2)}, u32[]{:S(2)}) async-start(f32[8,1,128]{2,1,0:T(1,128)} %bitcast.14), calls=%async_computation.2 | async-start | bytes 8192 | tf_op jit(solution)/shard_map/all_to_all | solution.py:206
  123.3 9.6 %copy-start.26 = (f32[1024]{0:T(1024)S(1)}, f32[1024]{0:T(1024)}, u32[]{:S(2)}) copy-start(f32[1024]{0:T(1024)} %get-tuple-element.119) | copy-start | bytes 12292
  123.3 10.7 %copy-start.22 = (s32[1024]{0:T(1024)S(1)}, s32[1024]{0:T(1024)}, u32[]{:S(2)}) copy-start(s32[1024]{0:T(1024)} %copy-done.21) | copy-start | bytes 12292
  123.3 21.8 %copy-start.18 = (f32[1024]{0:T(1024)S(1)}, f32[1024]{0:T(1024)}, u32[]{:S(2)}) copy-start(f32[1024]{0:T(1024)} %copy-done.17) | copy-start | bytes 12292
  140.9 8.9 %all-to-all-start.3 = ((f32[3,8,128]{2,0,1:T(4,128)}), f32[3,8,128]{2,0,1:T(4,128)S(1)}, u32[]{:S(2)}, u32[]{:S(2)}) async-start(f32[3,8,128]{2,0,1:T(4,128)} %copy.45), calls=%async_computation.3 | async-start | bytes 32768 | tf_op jit(solution)/shard_map/all_to_all | solution.py:222
  145.1 95.0 %all-reduce.3.cloned.1.call-start = ((), (), s32[]{:S(2)}) async-start(), calls=%async_computation.4 | async-start | bytes 4227072 | tf_op jit(solution)/shard_map/psum | solution.py:225
  240.1 5.7 %copy-start.25 = (f32[8,512]{1,0:T(8,128)S(1)}, f32[8,512]{1,0:T(8,128)}, u32[]{:S(2)}) copy-start(f32[8,512]{1,0:T(8,128)} %get-tuple-element.130) | copy-start | bytes 49156
  245.8 7.9 %copy-start.11 = (f32[1,1,8,512]{3,2,1,0:T(8,128)S(1)}, f32[1,1,8,512]{3,2,1,0:T(8,128)}, u32[]{:S(2)}) copy-start(f32[1,1,8,512]{3,2,1,0:T(8,128)} %get-tuple-element.155) | copy-start | bytes 49156
  245.8 7.9 %copy-start.12 = (f32[1,1,8,512]{3,2,1,0:T(8,128)S(1)}, f32[1,1,8,512]{3,2,1,0:T(8,128)}, u32[]{:S(2)}) copy-start(f32[1,1,8,512]{3,2,1,0:T(8,128)} %get-tuple-element.165) | copy-start | bytes 49156
  245.8 8.1 %copy-start.14 = (f32[5,1,8,512]{3,2,1,0:T(8,128)S(1)}, f32[5,1,8,512]{3,2,1,0:T(8,128)}, u32[]{:S(2)}) copy-start(f32[5,1,8,512]{3,2,1,0:T(8,128)} %copy-done.13) | copy-start | bytes 245764
  245.8 8.1 %copy-start.16 = (f32[5,1,8,512]{3,2,1,0:T(8,128)S(1)}, f32[5,1,8,512]{3,2,1,0:T(8,128)}, u32[]{:S(2)}) copy-start(f32[5,1,8,512]{3,2,1,0:T(8,128)} %copy-done.15) | copy-start | bytes 245764
  247.0 0.8 copy-start.7
  247.8 11.4 %collective-permute-start.4 = (f32[2,8,512]{2,1,0:T(8,128)S(1)}, f32[2,8,512]{2,1,0:T(8,128)S(1)}, u32[]{:S(2)}, u32[]{:S(2)}) collective-permute-start(f32[2,8,512]{2,1,0:T(8,128)S(1)} %get-tuple-element.213), channel_id=1, source_target_pairs={{1,0},{2,1},{3,2},{5,4},{6,5},{7,6},{9,8},{10,9},{11,10},{13,12},{... | collective-permute-start | bytes 98312 | tf_op jit(solution)/shard_map/ppermute | solution.py:44
  249.1 6.4 %collective-permute-start.5 = (f32[2,8,512]{2,1,0:T(8,128)S(1)}, f32[2,8,512]{2,1,0:T(8,128)S(1)}, u32[]{:S(2)}, u32[]{:S(2)}) collective-permute-start(f32[2,8,512]{2,1,0:T(8,128)S(1)} %get-tuple-element.214), channel_id=1, source_target_pairs={{0,1},{1,2},{2,3},{4,5},{5,6},{6,7},{8,9},{9,10},{10,11},{12,13},{... | collective-permute-start | bytes 98312 | tf_op jit(solution)/shard_map/ppermute | solution.py:43
  254.6 4.7 %copy-start.8 = (f32[32,8,512]{2,1,0:T(8,128)S(1)}, f32[32,8,512]{2,1,0:T(8,128)}, u32[]{:S(2)}) copy-start(f32[32,8,512]{2,1,0:T(8,128)} %copy-done.7) | copy-start | bytes 1572868
  255.5 11.9 %copy-start.28 = (f32[5]{0:T(128)S(1)}, f32[5]{0:T(128)}, u32[]{:S(2)}) copy-start(f32[5]{0:T(128)} %constant.174.clone) | copy-start | bytes 64
  256.5 10.9 %collective-permute-start.3 = (f32[5,2,12,512]{3,2,1,0:T(8,128)S(1)}, f32[5,2,12,512]{3,2,1,0:T(8,128)S(1)}, u32[]{:S(2)}, u32[]{:S(2)}) collective-permute-start(f32[5,2,12,512]{3,2,1,0:T(8,128)S(1)} %get-tuple-element.185), channel_id=1, source_target_pairs={{1,0},{2,1},{3,2},{0,3},{5,4},{6,5},{7,6},{4,7},{9,8},{10,9},{11,1... | collective-permute-start | bytes 737288 | tf_op jit(solution)/shard_map/ppermute | solution.py:44
  259.3 13.8 %collective-permute-start.2 = (f32[5,2,12,512]{3,2,1,0:T(8,128)S(1)}, f32[5,2,12,512]{3,2,1,0:T(8,128)S(1)}, u32[]{:S(2)}, u32[]{:S(2)}) collective-permute-start(f32[5,2,12,512]{3,2,1,0:T(8,128)S(1)} %get-tuple-element.184), channel_id=1, source_target_pairs={{0,1},{1,2},{2,3},{3,0},{4,5},{5,6},{6,7},{7,4},{8,9},{9,10},{10,1... | collective-permute-start | bytes 737288 | tf_op jit(solution)/shard_map/ppermute | solution.py:43
  273.6 1.6 copy-start.2
  300.7 4.9 %slice-start = ((s8[5898240]{0:T(1024)(128)(4,1)}), s8[4194304]{0:T(1024)(128)(4,1)S(1)}, s32[]{:S(2)}) async-start(s8[5898240]{0:T(1024)(128)(4,1)} %bitcast.65), calls=%async_computation.5 | async-start | bytes 8388608
  302.2 3.4 slice-start.1
  305.7 1.8 copy-start.3
  305.7 2.7 copy-start.4
  309.7 3.6 %copy-start.5 = (f32[5,32,12,512]{3,2,1,0:T(8,128)}, f32[5,32,12,512]{3,2,1,0:T(8,128)S(1)}, u32[]{:S(2)}) copy-start(f32[5,32,12,512]{3,2,1,0:T(8,128)S(1)} %get-tuple-element.180) | copy-start | bytes 11796484
  313.4 1.7 copy-start.1
  325.6 7.6 %copy-start.32 = (f32[5]{0:T(128)S(1)}, f32[5]{0:T(128)}, u32[]{:S(2)}) copy-start(f32[5]{0:T(128)} %constant.175) | copy-start | bytes 64
Sparse Core Ops, SparseCore 0:
  155.9 84.1 all-reduce.2
where the time goes:
time: 357 us; the launch traced here: 355 us
  waiting for transfers between devices  102 us (29%)
  local copies, waits for them, and re-layouts  93 us (26%)
  other arithmetic  85.4 us (24%)
  blocking collectives  32.5 us (9%)
  starting transfers between devices  27.2 us (8%)
  between operations  14.8 us (4%)
    psum x1, waiting for transfers between devices, shards(): wall_sums, column_total = lax.psum((dense_rows, slab_total), 'wall')  83.6 us
    scatter x1, local copies, waits for them, and re-layouts, shards(): padded_state = padded_state.at[:, :, 2:-2, :].set(inner_cols)  20.4 us
    psum x1, blocking collectives, from_root(): return lax.psum(kept, axis)  19.3 us
    add x1, other arithmetic, advance(): return center_state + time_step * (viscous - convect - sponge)  15.3 us
    unnamed x27, other arithmetic  13.4 us
    all_gather x1, blocking collectives, prefix(): pieces = lax.all_gather(value, axis)  13.3 us
    unnamed x83, local copies, waits for them, and re-layouts  11.8 us
    gather x1, local copies, waits for them, and re-layouts, shards(): recovery_ask = jnp.take(wall_fields[1], asked_cells)  10.5 us
  transfers between devices with their start and end apart: 11, of which 5 were waited for; matrix products, arithmetic and copies ran while one was open for 25% of the time, Pallas kernels for 0%

commit v1 on v0

v1 whole, which is shorter than its diff:
```python
import functools

import jax
import jax.numpy as jnp
from jax import lax
from jax.experimental import pallas as pl
from jax.experimental.pallas import tpu as pltpu
from jax.sharding import PartitionSpec as P

f32 = jnp.float32
bf16 = jnp.bfloat16
MESH = pl.DeviceIdType.MESH

time_step = 0.15
viscosity = 0.05
conduction = 0.07
sponge_rate = 0.5
far_values = (1.0, 0.5, 0.0, 0.0, 2.625)
SCALE = time_step / 12.0
CHUNK = 4


def parts3(x):
    a = x.astype(bf16).astype(f32)
    b = (x - a).astype(bf16).astype(f32)
    c = (x - a - b).astype(bf16).astype(f32)
    return a, b, c


def shift_of(n):
    assert n & (n - 1) == 0
    return n.bit_length() - 1


def pick(index, table_ref, count):
    out = jnp.zeros(index.shape, f32)
    for z in range(count):
        out = jnp.where(index == z, table_ref[z], out)
    return out


def normal_fields(density, vx, vy, vz, pressure):
    energy = 2.5 * pressure + 0.5 * density * (vx * vx + vy * vy + vz * vz)
    svz = SCALE * vz
    rho_w = density * svz
    flux = (
        rho_w,
        rho_w * vx,
        rho_w * vy,
        rho_w * vz + SCALE * pressure,
        (energy + pressure) * svz,
    )
    cv = SCALE * viscosity
    return flux, (cv * vx, cv * vy, cv * vz, (SCALE * conduction) * (pressure / density))


def primitives_of(u0, u1, u2, u3, u4):
    inv = 1.0 / u0
    vx, vy, vz = u1 * inv, u2 * inv, u3 * inv
    pressure = 0.4 * (u4 - 0.5 * (u1 * vx + u2 * vy + u3 * vz))
    return inv, vx, vy, vz, pressure


def kernel(
    dims,
    flow, spacing, kind, cells, zones, abl, conduct, diffuse, rate,
    out, shift_out, abl_out,
    F3, Q, XR, XL, RL, RR, PM, V, send_list, recv_list, reply, reply_in,
    slab_total, totals_in, film_buf, film_in, part, part_in,
    halo_u, halo_s, sp, dense,
    s_list, r_list, s_rep, r_rep, s_tot, r_tot, s_film, r_film, s_part, r_part,
    s_hu, r_hu, s_hs, r_hs, s_x, r_x,
):
    K, I, J, NT, W, C, PT, NZ = dims
    R = I * J // 128
    JB = J // 128
    s = lax.axis_index("surf")
    w = lax.axis_index("wall")
    barrier = pltpu.get_barrier_semaphore()
    for d in range(1, NT):
        pl.semaphore_signal(barrier, inc=1, device_id=(lax.rem(s + d, NT), w), device_id_type=MESH)
    for d in range(1, W):
        pl.semaphore_signal(barrier, inc=1, device_id=(s, lax.rem(w + d, W)), device_id_type=MESH)

    def add_total(k, total):
        layer = spacing[k]
        sp[k + 2] = layer
        return total + layer

    slab_total[...] = lax.fori_loop(0, K, add_total, jnp.zeros((I, J), f32))
    inv, vx, vy, vz, pressure = primitives_of(*[flow[e, 0] for e in range(5)])
    film_buf[0] = 2.0 / spacing[0]
    film_buf[1] = pressure * inv + 0.2 * (vx * vx + vy * vy + vz * vz)

    cell = cells[...]
    tile = lax.shift_right_logical(cell, shift_of(I * J))
    within = jnp.bitwise_and(cell, I * J - 1)
    row_i = lax.shift_right_logical(within, shift_of(J))
    col_j = jnp.bitwise_and(within, J - 1)
    row = lax.shift_right_logical(col_j, 7) * I + row_i
    lane = jnp.bitwise_and(col_j, 127)
    zone = zones[...]
    tile_iota = lax.broadcasted_iota(jnp.int32, (NT, C), 0)
    lane_iota = lax.broadcasted_iota(jnp.int32, (NT, C), 1)
    mine = jnp.where(tile_iota == tile, 1.0, 0.0).astype(f32)
    run = mine
    step = 1
    while step < C:
        run = run + jnp.where(lane_iota >= step, pltpu.roll(run, step, 1), 0.0)
        step *= 2
    rank = jnp.sum(mine * run, axis=0, keepdims=True).astype(jnp.int32) - 1
    slot = tile * PT + rank
    V[...] = jnp.zeros(V.shape, f32)
    V[0:1, 0:C] = row.astype(f32)
    V[1:2, 0:C] = lane.astype(f32)
    V[2:3, 0:C] = zone.astype(f32)
    for n, piece in enumerate(parts3(abl[0:1, :]) + parts3(abl[1:2, :])):
        V[3 + n : 4 + n, 0:C] = piece
    payload = V[:, 0:C].astype(bf16)
    slot_iota = lax.broadcasted_iota(jnp.int32, (PT, C), 0)
    for t in range(NT):
        block = jnp.where(slot_iota + t * PT == slot, 1.0, 0.0).astype(bf16)
        PM[t * PT : (t + 1) * PT, :] = block
        got = lax.dot_general(payload, block, (((1,), (1,)), ((), ())), preferred_element_type=f32)
        send_list[t] = jnp.zeros((8, PT), f32)
        send_list[t, 0:3] = got[0:3]
        send_list[t, 3:4] = got[3:4] + got[4:5] + got[5:6]
        send_list[t, 4:5] = got[6:7] + got[7:8] + got[8:9]

    pl.semaphore_wait(barrier, NT - 1 + W - 1)

    def list_copy(d):
        t = lax.rem(s + d, NT)
        return pltpu.make_async_remote_copy(
            send_list.at[t], recv_list.at[d], s_list.at[d], r_list.at[d],
            device_id=(t, w), device_id_type=MESH)

    def total_copy(d):
        return pltpu.make_async_remote_copy(
            slab_total, totals_in.at[w], s_tot.at[d], r_tot.at[d],
            device_id=(s, lax.rem(w + d, W)), device_id_type=MESH)

    def film_copy(d):
        return pltpu.make_async_remote_copy(
            film_buf, film_in, s_film.at[d], r_film,
            device_id=(s, lax.rem(w + d, W)), device_id_type=MESH)

    def halo_copies(side):
        near, target = (K - 2, lax.rem(w + 1, W)) if side == 0 else (0, lax.rem(w + W - 1, W))
        return (
            pltpu.make_async_remote_copy(
                flow.at[:, near : near + 2], halo_u.at[side], s_hu.at[side], r_hu.at[side],
                device_id=(s, target), device_id_type=MESH),
            pltpu.make_async_remote_copy(
                spacing.at[near : near + 2], halo_s.at[side], s_hs.at[side], r_hs.at[side],
                device_id=(s, target), device_id_type=MESH),
        )

    for d in range(1, NT):
        list_copy(d).start()

    @pl.when(w == 0)
    def _():
        for d in range(1, W):
            film_copy(d).start()

    for d in range(1, W):
        total_copy(d).start()
    totals_in[w] = slab_total[...]

    @pl.when(w < W - 1)
    def _():
        for copy in halo_copies(0):
            copy.start()

    @pl.when(w > 0)
    def _():
        for copy in halo_copies(1):
            copy.start()

    def side_copies(c):
        ks = pl.ds(c * CHUNK, CHUNK)
        return (
            pltpu.make_async_remote_copy(
                XR.at[ks], RL.at[ks], s_x.at[0, c], r_x.at[0, c],
                device_id=(lax.rem(s + 1, NT), w), device_id_type=MESH),
            pltpu.make_async_remote_copy(
                XL.at[ks], RR.at[ks], s_x.at[1, c], r_x.at[1, c],
                device_id=(lax.rem(s + NT - 1, NT), w), device_id_type=MESH),
        )

    i_row = lax.broadcasted_iota(jnp.int32, (I, J), 0)

    def surface_terms(k, carry):
        u = [flow[e, k] for e in range(5)]
        inv, vx, vy, vz, pressure = primitives_of(*u)
        enthalpy = u[4] + pressure
        sx, sy, sz, sp_ = SCALE * vx, SCALE * vy, SCALE * vz, SCALE * pressure
        m12, m13, m23 = u[1] * sy, u[1] * sz, u[2] * sz
        q = (viscosity * sx, viscosity * sy, viscosity * sz,
             (conduction * inv) * sp_)
        f1 = (SCALE * u[1], u[1] * sx + sp_, m12, m13, enthalpy * sx)
        f2 = (SCALE * u[2], m12, u[2] * sy + sp_, m23, enthalpy * sy)
        f3 = (SCALE * u[3], m13, m23, u[3] * sz + sp_, enthalpy * sz)
        for e in range(5):
            F3[k + 2, e] = f3[e]
        for e in range(4):
            Q[k + 2, e] = q[e]
        for e in range(5):
            total = u[e]
            if e:
                qe = q[e - 1]
                total = total - 60.0 * qe
                q8 = 8.0 * qe
            for axis, size, flux in ((0, I, f1[e]), (1, J, f2[e])):
                if e:
                    up2 = flux - qe
                    down2 = -flux - qe
                    up1 = q8 - 8.0 * up2
                    down1 = q8 - 8.0 * down2
                else:
                    up2 = flux
                    down2 = -flux
                    up1 = -8.0 * flux
                    down1 = 8.0 * flux
                r1 = pltpu.roll(down1, 1, axis)
                r2 = pltpu.roll(down2, 2, axis)
                l1 = pltpu.roll(up1, size - 1, axis)
                l2 = pltpu.roll(up2, size - 2, axis)
                if axis == 0:
                    to_right = r2 + jnp.where(i_row == 0, r1, 0.0)
                    to_left = up2 + jnp.where(i_row == 1, pltpu.roll(up1, 1, 0), 0.0)
                    XR[k, e] = to_right[0:2]
                    XL[k, e] = to_left[0:2]
                    r1 = jnp.where(i_row >= 1, r1, 0.0)
                    r2 = jnp.where(i_row >= 2, r2, 0.0)
                    l1 = jnp.where(i_row <= I - 2, l1, 0.0)
                    l2 = jnp.where(i_row <= I - 3, l2, 0.0)
                total = total + ((r1 + r2) + (l1 + l2))
            out[e, k] = total
        return carry

    for c in range(K // CHUNK):
        lax.fori_loop(c * CHUNK, (c + 1) * CHUNK, surface_terms, 0)
        for copy in side_copies(c):
            copy.start()

    recv_list[0] = send_list[s]
    for d in range(1, NT):
        list_copy(d).wait()
    listed = jnp.concatenate([recv_list[d] for d in range(NT)], axis=1)
    count = NT * PT
    l_row = listed[0:1].astype(jnp.int32)
    l_lane = listed[1:2].astype(jnp.int32)
    row_hot = jnp.where(lax.broadcasted_iota(jnp.int32, (R, count), 0) == l_row, 1.0, 0.0)
    lane_hot = jnp.where(
        lax.broadcasted_iota(jnp.int32, (128, count), 0) == l_lane, 1.0, 0.0).astype(bf16)
    pieces = parts3(listed[3:4]) + parts3(listed[4:5]) + (listed[2:3],)
    stack = jnp.concatenate([row_hot * piece for piece in pieces], axis=0).astype(bf16)
    grid = lax.dot_general(stack, lane_hot, (((1,), (1,)), ((), ())), preferred_element_type=f32)
    first = grid[0:R] + grid[R : 2 * R] + grid[2 * R : 3 * R]
    second = grid[3 * R : 4 * R] + grid[4 * R : 5 * R] + grid[5 * R : 6 * R]
    zone_grid = grid[6 * R : 7 * R]

    @pl.when(w == 0)
    def _():
        for d in range(1, W):
            film_copy(d).wait_send()
        film_in[...] = film_buf[...]

    @pl.when(w > 0)
    def _():
        film_copy(1).wait_recv()

    film = jnp.concatenate([film_in[0, :, b * 128 : (b + 1) * 128] for b in range(JB)], axis=0)
    recov = jnp.concatenate([film_in[1, :, b * 128 : (b + 1) * 128] for b in range(JB)], axis=0)
    zone_grid = zone_grid.astype(jnp.int32)
    owned = first > 0.25
    cond = pick(zone_grid, conduct, NZ)
    surface = jnp.where(owned, first, 1.0)
    for newton_pass in range(2):
        cube = surface * surface * surface
        surface = (film * recov + cond * second + 2.4 * cube * surface) / (film + cond + 3.2 * cube)
    recess = pick(zone_grid, rate, NZ) * jnp.exp(-2.0 / surface)
    part[0] = jnp.where(owned, surface, 0.0)
    part[1] = jnp.where(owned, recess, 0.0)

    def part_copy(d):
        return pltpu.make_async_remote_copy(
            part, part_in.at[d], s_part.at[d], r_part.at[d],
            device_id=(s, lax.rem(w + d, W)), device_id_type=MESH)

    for d in range(1, W):
        part_copy(d).start()

    table = jnp.concatenate(parts3(part[0]), axis=0).astype(bf16)
    spread = jnp.dot(table, lane_hot, preferred_element_type=f32)
    spread = spread[0:R] + spread[R : 2 * R] + spread[2 * R : 3 * R]
    answer = jnp.sum(spread * row_hot, axis=0, keepdims=True)
    for d in range(NT):
        reply[d] = jnp.broadcast_to(answer[:, d * PT : (d + 1) * PT], (8, PT))

    def reply_copy(d):
        return pltpu.make_async_remote_copy(
            reply.at[d], reply_in.at[s], s_rep.at[d], r_rep.at[d],
            device_id=(lax.rem(s + NT - d, NT), w), device_id_type=MESH)

    for d in range(1, NT):
        reply_copy(d).start()
    reply_in[s] = reply[0]

    for d in range(1, W):
        part_copy(d).wait()
    whole = part[...]
    for d in range(1, W):
        whole = whole + part_in[d]
    dense[...] = whole
    surf_temp = jnp.concatenate([dense[0, b * I : (b + 1) * I, :] for b in range(JB)], axis=1)
    surf_recess = jnp.concatenate([dense[1, b * I : (b + 1) * I, :] for b in range(JB)], axis=1)

    for d in range(1, W):
        total_copy(d).wait()
    column_total = jnp.zeros((I, J), f32)
    offset = jnp.zeros((I, J), f32)
    for n in range(W):
        column_total = column_total + totals_in[n]
        offset = offset + jnp.where(n < w, totals_in[n], 0.0)

    @pl.when(w < W - 1)
    def _():
        for copy in halo_copies(0):
            copy.wait_send()
        for copy in halo_copies(1):
            copy.wait_recv()

    @pl.when(w > 0)
    def _():
        for copy in halo_copies(1):
            copy.wait_send()
        for copy in halo_copies(0):
            copy.wait_recv()

    def put(at, values):
        flux, fields = values
        for e in range(5):
            F3[at, e] = flux[e]
        for e in range(4):
            Q[at, e] = fields[e]

    def put_halo(side, base):
        for n in range(2):
            u = [halo_u[side, e, n] for e in range(5)]
            inv, vx, vy, vz, pressure = primitives_of(*u)
            put(base + n, normal_fields(u[0], vx, vy, vz, pressure))
            sp[base + n] = halo_s[side, n]

    @pl.when(w > 0)
    def _():
        put_halo(0, 0)

    @pl.when(w < W - 1)
    def _():
        put_halo(1, K + 2)

    @pl.when(w == 0)
    def _():
        kinds = kind[...]
        slip = kinds == 1
        for n in range(2):
            u = [flow[e, n] for e in range(5)]
            inv, vx, vy, vz, pressure = primitives_of(*u)
            density = jnp.where(slip, u[0], pressure / surf_temp)
            vx = jnp.where(slip, vx, -vx)
            vy = jnp.where(slip, vy, -vy)
            vz = jnp.where(kinds == 2, 2.0 * surf_recess - vz, -vz)
            put(1 - n, normal_fields(density, vx, vy, vz, pressure))
        sp[1] = spacing[1]
        sp[0] = spacing[0]

    @pl.when(w == W - 1)
    def _():
        one = jnp.full((I, J), 1.0, f32)
        zero = jnp.zeros((I, J), f32)
        for n in range(2):
            put(K + 2 + n, normal_fields(one, 0.5 * one, zero, zero, one))
        sp[K + 2] = spacing[K - 2]
        sp[K + 3] = spacing[K - 1]

    inv_total = 1.0 / column_total
    stretch = (1.0 + surf_recess * inv_total) * (1.0 / 12.0)

    def normal_terms(k, run):
        here = sp[k + 2]
        metric = stretch * (
            3.0 * (sp[k + 1] + sp[k + 3]) + 7.0 * here - 0.5 * (sp[k] + sp[k + 4]))
        inv_metric = 1.0 / metric
        inv_square = inv_metric * inv_metric
        normalized = (run + 0.5 * here) * inv_total
        shift_out[k] = surf_recess * (normalized - 1.0)
        damp = (time_step * sponge_rate) * normalized * normalized
        for e in range(5):
            diff = 8.0 * (F3[k + 3, e] - F3[k + 1, e]) - (F3[k + 4, e] - F3[k, e])
            total = out[e, k] - inv_metric * diff - damp * (flow[e, k] - far_values[e])
            if e:
                lap = (16.0 * (Q[k + 3, e - 1] + Q[k + 1, e - 1])
                       - (Q[k + 4, e - 1] + Q[k, e - 1]) - 30.0 * Q[k + 2, e - 1])
                total = total + inv_square * lap
            out[e, k] = total
        return run + here

    lax.fori_loop(0, K, normal_terms, offset)

    for d in range(1, NT):
        reply_copy(d).wait()
    answer = jnp.concatenate([reply_in[t, 0:1] for t in range(NT)], axis=1)
    V[...] = jnp.zeros(V.shape, f32)
    for n, piece in enumerate(parts3(answer)):
        V[n : n + 1, 0:count] = piece
    back = jnp.dot(V[:, 0:count].astype(bf16), PM[...], preferred_element_type=f32)
    col_surface = back[0:1] + back[1:2] + back[2:3]
    col_diffuse = pick(zone, diffuse, NZ)
    depth = abl.shape[0]
    depth_row = lax.broadcasted_iota(jnp.int32, (depth, C), 0)
    profile = jnp.where(depth_row == 0, col_surface, abl[...])
    for heat_pass in range(2):
        below = pltpu.roll(profile, 1, 0)
        above = jnp.where(depth_row == depth - 1, below, pltpu.roll(profile, depth - 1, 0))
        gain = col_diffuse * (above - 2.0 * profile + below)
        profile = jnp.where(depth_row == 0, profile, profile + gain)
    abl_out[...] = profile

    def add_sides(k, carry):
        for e in range(5):
            out[e, k, 0:2] = out[e, k, 0:2] + RL[k, e]
            out[e, k, I - 2 : I] = out[e, k, I - 2 : I] + RR[k, e]
        return carry

    for c in range(K // CHUNK):
        for copy in side_copies(c):
            copy.wait()
        lax.fori_loop(c * CHUNK, (c + 1) * CHUNK, add_sides, 0)


def shards(flow_state, spacing, bc_kind, cell_of, zone_id, abl_temp, conduct, diffuse, rate):
    NT = lax.axis_size("surf")
    W = lax.axis_size("wall")
    K, I, J = spacing.shape
    C = cell_of.shape[0]
    PT = -(-(C // NT) // 128) * 128
    R = I * J // 128
    count = NT * PT
    dims = (K, I, J, NT, W, C, PT, conduct.shape[0])
    vmem = pl.BlockSpec(memory_space=pltpu.VMEM)
    smem = pl.BlockSpec(memory_space=pltpu.SMEM)
    dma = pltpu.SemaphoreType.DMA
    chunks = K // CHUNK
    scratch = [
        pltpu.VMEM((K + 4, 5, I, J), f32),
        pltpu.VMEM((K + 4, 4, I, J), f32),
        pltpu.VMEM((K, 5, 2, J), f32),
        pltpu.VMEM((K, 5, 2, J), f32),
        pltpu.VMEM((K, 5, 2, J), f32),
        pltpu.VMEM((K, 5, 2, J), f32),
        pltpu.VMEM((count, C), bf16),
        pltpu.VMEM((16, max(C, count)), f32),
        pltpu.VMEM((NT, 8, PT), f32),
        pltpu.VMEM((NT, 8, PT), f32),
        pltpu.VMEM((NT, 8, PT), f32),
        pltpu.VMEM((NT, 8, PT), f32),
        pltpu.VMEM((I, J), f32),
        pltpu.VMEM((W, I, J), f32),
        pltpu.VMEM((2, I, J), f32),
        pltpu.VMEM((2, I, J), f32),
        pltpu.VMEM((2, R, 128), f32),
        pltpu.VMEM((W, 2, R, 128), f32),
        pltpu.VMEM((2, 5, 2, I, J), f32),
        pltpu.VMEM((2, 2, I, J), f32),
        pltpu.VMEM((K + 4, I, J), f32),
        pltpu.VMEM((2, R, 128), f32),
        dma((NT,)), dma((NT,)), dma((NT,)), dma((NT,)),
        dma((W,)), dma((W,)), dma((W,)), dma,
        dma((W,)), dma((W,)),
        dma((2,)), dma((2,)), dma((2,)), dma((2,)),
        dma((2, chunks)), dma((2, chunks)),
    ]
    return pl.pallas_call(
        functools.partial(kernel, dims),
        out_shape=(
            jax.ShapeDtypeStruct(flow_state.shape, f32),
            jax.ShapeDtypeStruct(spacing.shape, f32),
            jax.ShapeDtypeStruct(abl_temp.shape, f32),
        ),
        in_specs=[vmem] * 6 + [smem] * 3,
        out_specs=(vmem,) * 3,
        scratch_shapes=scratch,
        compiler_params=pltpu.CompilerParams(
            collective_id=0, has_side_effects=True, vmem_limit_bytes=50 * 1024 * 1024),
    )(flow_state, spacing, bc_kind, cell_of.reshape(1, C), zone_id.reshape(1, C), abl_temp,
      conduct, diffuse, rate)


def solution(mesh):
    in_specs = (
        P(None, "wall", "surf", None),
        P("wall", "surf", None),
        P("surf", None),
        P(("surf", "wall")),
        P(("surf", "wall")),
        P(None, ("surf", "wall")),
        P(),
        P(),
        P(),
    )
    out_specs = (P(None, "wall", "surf", None), P("wall", "surf", None), P(None, ("surf", "wall")))
    return jax.shard_map(shards, mesh=mesh, in_specs=in_specs, out_specs=out_specs, check_vma=False)
```

time: 357 us -> 40.8 us (0.11)
  waiting for transfers between devices: 102 us -> 0 us
  other arithmetic: 85.4 us -> 0 us
  local copies, waits for them, and re-layouts: 93 us -> 11.2 us
  blocking collectives: 32.5 us -> 0 us
  Pallas kernels: 0 us -> 28.6 us
  starting transfers between devices: 27.2 us -> 0 us
  between operations: 14.8 us -> 0.66 us
    psum x1 -> x0, waiting for transfers between devices: 83.6 us -> none  [shards(): wall_sums, column_total = lax.psum((dense_rows, slab_total), 'wall')]
    gather x6 -> x0, local copies, waits for them, and re-layouts: 48.5 us -> none  [the longest x1 10.5 us: shards(): recovery_ask = jnp.take(wall_fields[1], asked_cells)]
    pallas_call x0 -> x1, Pallas kernels: none -> 28.6 us  [shards(): pl.pallas_call(functools.partial(kernel, dims), out_shape=(jax.ShapeDtype...]
    add x6 -> x0, other arithmetic: 27.7 us -> none  [the longest x1 15.3 us: advance(): return center_state + time_step * (viscous - convect - sponge)]
    scatter x2 -> x0, local copies, waits for them, and re-layouts: 25.3 us -> none  [the longest x1 20.4 us: shards(): padded_state = padded_state.at[:, :, 2:-2, :].set(inner_cols)]
    psum x1 -> x0, blocking collectives: 19.3 us -> none  [from_root(): return lax.psum(kept, axis)]
    all_to_all x4 -> x0, starting transfers between devices: 15.9 us -> none  [the longest x1 5.17 us: shards(): lax.all_to_all(sorted_cells, 'surf', split_axis=0, concat_axis=0, tiled=T...]
    unnamed x27 -> x0, other arithmetic: 13.4 us -> none
  transfers between devices with their start and end apart: 11 -> 0, of which waited for: 5 -> 0; matrix products, arithmetic and copies ran while one was open for 25% -> 0% of each run, Pallas kernels for 0% -> 0%
where the time goes in v1:
time: 40.8 us; the launch traced here: 40.4 us
  Pallas kernels  28.6 us (70%)
  local copies, waits for them, and re-layouts  11.2 us (27%)
  between operations  0.66 us (2%)
    pallas_call x1, Pallas kernels, shards(): pl.pallas_call(functools.partial(kernel, dims), out_shape=(jax.ShapeDtype...  28.6 us
    unnamed x19, local copies, waits for them, and re-layouts  11.2 us

profile of v1, /device:TPU:0, one launch (start us, length us, event | category | flops | bytes accessed | tf_op | source)
XLA Modules:
  0.0 40.4 jit_solution(16564024939027984047)
XLA Ops:
  0.6 0.0 copy-start
  0.6 1.0 %copy-done = f32[32,8,512]{2,1,0:T(8,128)S(1)} copy-done((f32[32,8,512]{2,1,0:T(8,128)S(1)}, f32[32,8,512]{2,1,0:T(8,128)}, u32[]{:S(2)}) %copy-start) | copy-done | bytes 524312
  1.7 0.0 copy-start.1
  1.7 0.9 %copy-done.1 = f32[64,1024]{1,0:T(8,128)S(1)} copy-done((f32[64,1024]{1,0:T(8,128)S(1)}, f32[64,1024]{1,0:T(8,128)}, u32[]{:S(2)}) %copy-start.1) | copy-done | bytes 262168
  2.6 0.0 copy-start.2
  2.6 0.7 %copy-done.2 = s32[8,512]{1,0:T(8,128)S(1)} copy-done((s32[8,512]{1,0:T(8,128)S(1)}, s32[8,512]{1,0:T(8,128)}, u32[]{:S(2)}) %copy-start.2) | copy-done | bytes 16408
  3.3 0.0 copy-start.3
  3.3 0.7 %copy-done.3 = s32[1024]{0:T(1024)S(1)} copy-done((s32[1024]{0:T(1024)S(1)}, s32[1024]{0:T(1024)}, u32[]{:S(2)}) %copy-start.3) | copy-done | bytes 4120
  4.0 0.0 copy-start.4
  4.0 0.7 %copy-done.4 = s32[1024]{0:T(1024)S(1)} copy-done((s32[1024]{0:T(1024)S(1)}, s32[1024]{0:T(1024)}, u32[]{:S(2)}) %copy-start.4) | copy-done | bytes 4120
  4.7 0.0 copy-start.5
  4.7 0.7 %copy-done.5 = f32[8]{0:T(128)S(1)} copy-done((f32[8]{0:T(128)S(1)}, f32[8]{0:T(128)}, u32[]{:S(2)}) %copy-start.5) | copy-done | bytes 56
  5.4 0.0 copy-start.6
  5.4 0.7 %copy-done.6 = f32[8]{0:T(128)S(1)} copy-done((f32[8]{0:T(128)S(1)}, f32[8]{0:T(128)}, u32[]{:S(2)}) %copy-start.6) | copy-done | bytes 56
  6.0 0.0 copy-start.7
  6.0 0.7 %copy-done.7 = f32[8]{0:T(128)S(1)} copy-done((f32[8]{0:T(128)S(1)}, f32[8]{0:T(128)}, u32[]{:S(2)}) %copy-start.7) | copy-done | bytes 56
  6.7 28.6 %shard_map.112 = (f32[5,32,8,512]{3,2,1,0:T(8,128)}, f32[32,8,512]{2,1,0:T(8,128)S(1)}, f32[64,1024]{1,0:T(8,128)S(1)}) custom-call(f32[5,32,8,512]{3,2,1,0:T(8,128)} %flow.1, f32[32,8,512]{2,1,0:T(8,128)S(1)} %copy-done, s32[8,512]{1,0:T(8,128)S(1)} %copy-done.2, s32[1,1024]{1,0:T(1,128)S(1)} %bitcast.2, s32[1,1024]{1,0:T(1,128)S(1)} %bitcast.3, ...), custom_call_target="tpu_custom_call" | custom-call | tf_op jit(solution)/shard_map/pallas_call | solution.py:486
  35.3 3.6 %copy.15 = f32[5,32,8,512]{3,2,1,0:T(8,128)} copy(f32[5,32,8,512]{3,2,1,0:T(8,128)} %get-tuple-element.6) | data formatting | bytes 5242880
  38.9 0.8 %copy.16 = f32[32,8,512]{2,1,0:T(8,128)} copy(f32[32,8,512]{2,1,0:T(8,128)S(1)} %get-tuple-element.7) | data formatting | bytes 1048576
  39.7 0.7 %copy.17 = f32[64,1024]{1,0:T(8,128)} copy(f32[64,1024]{1,0:T(8,128)S(1)} %get-tuple-element.8) | data formatting | bytes 524288
Async XLA Ops:
  0.6 1.0 %copy-start = (f32[32,8,512]{2,1,0:T(8,128)S(1)}, f32[32,8,512]{2,1,0:T(8,128)}, u32[]{:S(2)}) copy-start(f32[32,8,512]{2,1,0:T(8,128)} %spacing.1) | copy-start | bytes 1572868
  1.7 0.9 %copy-start.1 = (f32[64,1024]{1,0:T(8,128)S(1)}, f32[64,1024]{1,0:T(8,128)}, u32[]{:S(2)}) copy-start(f32[64,1024]{1,0:T(8,128)} %abl.1) | copy-start | bytes 786436
  2.6 0.7 %copy-start.2 = (s32[8,512]{1,0:T(8,128)S(1)}, s32[8,512]{1,0:T(8,128)}, u32[]{:S(2)}) copy-start(s32[8,512]{1,0:T(8,128)} %kind.1) | copy-start | bytes 49156
  3.3 0.7 %copy-start.3 = (s32[1024]{0:T(1024)S(1)}, s32[1024]{0:T(1024)}, u32[]{:S(2)}) copy-start(s32[1024]{0:T(1024)} %param.12) | copy-start | bytes 12292
  4.0 0.7 %copy-start.4 = (s32[1024]{0:T(1024)S(1)}, s32[1024]{0:T(1024)}, u32[]{:S(2)}) copy-start(s32[1024]{0:T(1024)} %param.13) | copy-start | bytes 12292
  4.7 0.7 %copy-start.5 = (f32[8]{0:T(128)S(1)}, f32[8]{0:T(128)}, u32[]{:S(2)}) copy-start(f32[8]{0:T(128)} %conduct.1) | copy-start | bytes 100
  5.4 0.7 %copy-start.6 = (f32[8]{0:T(128)S(1)}, f32[8]{0:T(128)}, u32[]{:S(2)}) copy-start(f32[8]{0:T(128)} %diffuse.1) | copy-start | bytes 100
  6.0 0.7 %copy-start.7 = (f32[8]{0:T(128)S(1)}, f32[8]{0:T(128)}, u32[]{:S(2)}) copy-start(f32[8]{0:T(128)} %rate.1) | copy-start | bytes 100

commit v2 on v1

--- a/solution.py
+++ b/solution.py
@@ -18,6 +18,8 @@
 far_values = (1.0, 0.5, 0.0, 0.0, 2.625)
 SCALE = time_step / 12.0
 CHUNK = 4
+VMEM_BYTES = 62 * 1024 * 1024
+PIECES = 2
 
 
 def parts3(x):
@@ -63,8 +65,10 @@
 
 def kernel(
     dims,
-    flow, spacing, kind, cells, zones, abl, conduct, diffuse, rate,
-    out, shift_out, abl_out,
+    flow_hbm, spacing_hbm, kind_hbm, cells_hbm, zones_hbm, abl_hbm, conduct_hbm, diffuse_hbm, rate_hbm,
+    out_hbm, shift_hbm, abl_out_hbm,
+    out, shift_out, abl_out, s_out,
+    flow, spacing, kind, cells, zones, abl, conduct, diffuse, rate, s_flow, s_in,
     F3, Q, XR, XL, RL, RR, PM, V, send_list, recv_list, reply, reply_in,
     slab_total, totals_in, film_buf, film_in, part, part_in,
     halo_u, halo_s, sp, dense,
@@ -76,59 +80,25 @@
     JB = J // 128
     s = lax.axis_index("surf")
     w = lax.axis_index("wall")
+
+    def flow_copy(c):
+        ks = pl.ds(c * CHUNK, CHUNK)
+        return pltpu.make_async_copy(flow_hbm.at[:, ks], flow.at[:, ks], s_flow.at[c])
+
+    pairs = ((spacing_hbm, spacing), (cells_hbm, cells), (zones_hbm, zones), (abl_hbm, abl),
+             (kind_hbm, kind), (conduct_hbm, conduct), (diffuse_hbm, diffuse), (rate_hbm, rate))
+    inputs = [pltpu.make_async_copy(a, b, s_in.at[n]) for n, (a, b) in enumerate(pairs)]
+    flow_copy(0).start()
+    for copy in inputs:
+        copy.start()
+    for c in range(1, K // CHUNK):
+        flow_copy(c).start()
     barrier = pltpu.get_barrier_semaphore()
     for d in range(1, NT):
         pl.semaphore_signal(barrier, inc=1, device_id=(lax.rem(s + d, NT), w), device_id_type=MESH)
     for d in range(1, W):
         pl.semaphore_signal(barrier, inc=1, device_id=(s, lax.rem(w + d, W)), device_id_type=MESH)
 
-    def add_total(k, total):
-        layer = spacing[k]
-        sp[k + 2] = layer
-        return total + layer
-
-    slab_total[...] = lax.fori_loop(0, K, add_total, jnp.zeros((I, J), f32))
-    inv, vx, vy, vz, pressure = primitives_of(*[flow[e, 0] for e in range(5)])
-    film_buf[0] = 2.0 / spacing[0]
-    film_buf[1] = pressure * inv + 0.2 * (vx * vx + vy * vy + vz * vz)
-
-    cell = cells[...]
-    tile = lax.shift_right_logical(cell, shift_of(I * J))
-    within = jnp.bitwise_and(cell, I * J - 1)
-    row_i = lax.shift_right_logical(within, shift_of(J))
-    col_j = jnp.bitwise_and(within, J - 1)
-    row = lax.shift_right_logical(col_j, 7) * I + row_i
-    lane = jnp.bitwise_and(col_j, 127)
-    zone = zones[...]
-    tile_iota = lax.broadcasted_iota(jnp.int32, (NT, C), 0)
-    lane_iota = lax.broadcasted_iota(jnp.int32, (NT, C), 1)
-    mine = jnp.where(tile_iota == tile, 1.0, 0.0).astype(f32)
-    run = mine
-    step = 1
-    while step < C:
-        run = run + jnp.where(lane_iota >= step, pltpu.roll(run, step, 1), 0.0)
-        step *= 2
-    rank = jnp.sum(mine * run, axis=0, keepdims=True).astype(jnp.int32) - 1
-    slot = tile * PT + rank
-    V[...] = jnp.zeros(V.shape, f32)
-    V[0:1, 0:C] = row.astype(f32)
-    V[1:2, 0:C] = lane.astype(f32)
-    V[2:3, 0:C] = zone.astype(f32)
-    for n, piece in enumerate(parts3(abl[0:1, :]) + parts3(abl[1:2, :])):
-        V[3 + n : 4 + n, 0:C] = piece
-    payload = V[:, 0:C].astype(bf16)
-    slot_iota = lax.broadcasted_iota(jnp.int32, (PT, C), 0)
-    for t in range(NT):
-        block = jnp.where(slot_iota + t * PT == slot, 1.0, 0.0).astype(bf16)
-        PM[t * PT : (t + 1) * PT, :] = block
-        got = lax.dot_general(payload, block, (((1,), (1,)), ((), ())), preferred_element_type=f32)
-        send_list[t] = jnp.zeros((8, PT), f32)
-        send_list[t, 0:3] = got[0:3]
-        send_list[t, 3:4] = got[3:4] + got[4:5] + got[5:6]
-        send_list[t, 4:5] = got[6:7] + got[7:8] + got[8:9]
-
-    pl.semaphore_wait(barrier, NT - 1 + W - 1)
-
     def list_copy(d):
         t = lax.rem(s + d, NT)
         return pltpu.make_async_remote_copy(
@@ -149,34 +119,12 @@
         near, target = (K - 2, lax.rem(w + 1, W)) if side == 0 else (0, lax.rem(w + W - 1, W))
         return (
             pltpu.make_async_remote_copy(
-                flow.at[:, near : near + 2], halo_u.at[side], s_hu.at[side], r_hu.at[side],
+                flow_hbm.at[:, near : near + 2], halo_u.at[side], s_hu.at[side], r_hu.at[side],
                 device_id=(s, target), device_id_type=MESH),
             pltpu.make_async_remote_copy(
-                spacing.at[near : near + 2], halo_s.at[side], s_hs.at[side], r_hs.at[side],
+                spacing_hbm.at[near : near + 2], halo_s.at[side], s_hs.at[side], r_hs.at[side],
                 device_id=(s, target), device_id_type=MESH),
         )
-
-    for d in range(1, NT):
-        list_copy(d).start()
-
-    @pl.when(w == 0)
-    def _():
-        for d in range(1, W):
-            film_copy(d).start()
-
-    for d in range(1, W):
-        total_copy(d).start()
-    totals_in[w] = slab_total[...]
-
-    @pl.when(w < W - 1)
-    def _():
-        for copy in halo_copies(0):
-            copy.start()
-
-    @pl.when(w > 0)
-    def _():
-        for copy in halo_copies(1):
-            copy.start()
 
     def side_copies(c):
         ks = pl.ds(c * CHUNK, CHUNK)
@@ -240,10 +188,92 @@
             out[e, k] = total
         return carry
 
-    for c in range(K // CHUNK):
+    def chunk(c, send=True):
+        flow_copy(c).wait()
         lax.fori_loop(c * CHUNK, (c + 1) * CHUNK, surface_terms, 0)
-        for copy in side_copies(c):
+        if send:
+            for copy in side_copies(c):
+                copy.start()
+
+    chunk(0, send=False)
+    pl.semaphore_wait(barrier, NT - 1 + W - 1)
+    for copy in side_copies(0):
+        copy.start()
+    @pl.when(w < W - 1)
+    def _():
+        for copy in halo_copies(0):
             copy.start()
+
+    @pl.when(w > 0)
+    def _():
+        for copy in halo_copies(1):
+            copy.start()
+
+    chunk(1)
+    inputs[0].wait()
+    def add_total(k, total):
+        layer = spacing[k]
+        sp[k + 2] = layer
+        return total + layer
+
+    slab_total[...] = lax.fori_loop(0, K, add_total, jnp.zeros((I, J), f32))
+    inv, vx, vy, vz, pressure = primitives_of(*[flow[e, 0] for e in range(5)])
+    film_buf[0] = 2.0 / spacing[0]
+    film_buf[1] = pressure * inv + 0.2 * (vx * vx + vy * vy + vz * vz)
+
+    @pl.when(w == 0)
+    def _():
+        for d in range(1, W):
+            film_copy(d).start()
+
+    for d in range(1, W):
+        total_copy(d).start()
+    totals_in[w] = slab_total[...]
+
+    chunk(2)
+
+    for copy in inputs[1:]:
+        copy.wait()
+    cell = cells[...]
+    tile = lax.shift_right_logical(cell, shift_of(I * J))
+    within = jnp.bitwise_and(cell, I * J - 1)
+    row_i = lax.shift_right_logical(within, shift_of(J))
+    col_j = jnp.bitwise_and(within, J - 1)
+    row = lax.shift_right_logical(col_j, 7) * I + row_i
+    lane = jnp.bitwise_and(col_j, 127)
+    zone = zones[...]
+    tile_iota = lax.broadcasted_iota(jnp.int32, (NT, C), 0)
+    lane_iota = lax.broadcasted_iota(jnp.int32, (NT, C), 1)
+    mine = jnp.where(tile_iota == tile, 1.0, 0.0).astype(f32)
+    run = mine
+    step = 1
+    while step < C:
+        run = run + jnp.where(lane_iota >= step, pltpu.roll(run, step, 1), 0.0)
+        step *= 2
+    rank = jnp.sum(mine * run, axis=0, keepdims=True).astype(jnp.int32) - 1
+    slot = tile * PT + rank
+    V[...] = jnp.zeros(V.shape, f32)
+    V[0:1, 0:C] = row.astype(f32)
+    V[1:2, 0:C] = lane.astype(f32)
+    V[2:3, 0:C] = zone.astype(f32)
+    for n, piece in enumerate(parts3(abl[0:1, :]) + parts3(abl[1:2, :])):
+        V[3 + n : 4 + n, 0:C] = piece
+    payload = V[:, 0:C].astype(bf16)
+    slot_iota = lax.broadcasted_iota(jnp.int32, (PT, C), 0)
+    for t in range(NT):
+        block = jnp.where(slot_iota + t * PT == slot, 1.0, 0.0).astype(bf16)
+        PM[t * PT : (t + 1) * PT, :] = block
+        got = lax.dot_general(payload, block, (((1,), (1,)), ((), ())), preferred_element_type=f32)
+        send_list[t] = jnp.zeros((8, PT), f32)
+        send_list[t, 0:3] = got[0:3]
+        send_list[t, 3:4] = got[3:4] + got[4:5] + got[5:6]
+        send_list[t, 4:5] = got[6:7] + got[7:8] + got[8:9]
+
+    for d in range(1, NT):
+        list_copy(d).start()
+
+    for c in (3, 4, 5):
+        chunk(c)
 
     recv_list[0] = send_list[s]
     for d in range(1, NT):
@@ -308,6 +338,8 @@
     for d in range(1, NT):
         reply_copy(d).start()
     reply_in[s] = reply[0]
+    for c in range(6, K // CHUNK):
+        chunk(c)
 
     for d in range(1, W):
         part_copy(d).wait()
@@ -409,6 +441,8 @@
         return run + here
 
     lax.fori_loop(0, K, normal_terms, offset)
+    shift_copy = pltpu.make_async_copy(shift_out, shift_hbm, s_out.at[0])
+    shift_copy.start()
 
     for d in range(1, NT):
         reply_copy(d).wait()
@@ -428,6 +462,8 @@
         gain = col_diffuse * (above - 2.0 * profile + below)
         profile = jnp.where(depth_row == 0, profile, profile + gain)
     abl_out[...] = profile
+    abl_copy = pltpu.make_async_copy(abl_out, abl_out_hbm, s_out.at[1])
+    abl_copy.start()
 
     def add_sides(k, carry):
         for e in range(5):
@@ -435,10 +471,32 @@
             out[e, k, I - 2 : I] = out[e, k, I - 2 : I] + RR[k, e]
         return carry
 
+    def out_copy(c):
+        ks = pl.ds(c * CHUNK, CHUNK)
+        return pltpu.make_async_copy(out.at[:, ks], out_hbm.at[:, ks], s_out.at[2 + c])
+
     for c in range(K // CHUNK):
         for copy in side_copies(c):
             copy.wait()
         lax.fori_loop(c * CHUNK, (c + 1) * CHUNK, add_sides, 0)
+        out_copy(c).start()
+    shift_copy.wait()
+    abl_copy.wait()
+    for c in range(K // CHUNK):
+        out_copy(c).wait()
+
+
+def hand_out(a, b, c, to_a, to_b, to_c, sem):
+    half = a.shape[1] // PIECES
+    copies = [pltpu.make_async_copy(b, to_b, sem.at[0]), pltpu.make_async_copy(c, to_c, sem.at[1])]
+    for e in range(a.shape[0]):
+        for n in range(PIECES):
+            ks = pl.ds(n * half, half)
+            copies.append(pltpu.make_async_copy(a.at[e, ks], to_a.at[e, ks], sem.at[len(copies)]))
+    for copy in copies:
+        copy.start()
+    for copy in copies:
+        copy.wait()
 
 
 def shards(flow_state, spacing, bc_kind, cell_of, zone_id, abl_temp, conduct, diffuse, rate):
@@ -450,11 +508,23 @@
     R = I * J // 128
     count = NT * PT
     dims = (K, I, J, NT, W, C, PT, conduct.shape[0])
-    vmem = pl.BlockSpec(memory_space=pltpu.VMEM)
-    smem = pl.BlockSpec(memory_space=pltpu.SMEM)
     dma = pltpu.SemaphoreType.DMA
     chunks = K // CHUNK
     scratch = [
+        pltpu.VMEM(flow_state.shape, f32),
+        pltpu.VMEM(spacing.shape, f32),
+        pltpu.VMEM(abl_temp.shape, f32),
+        dma((chunks + 2,)),
+        pltpu.VMEM(flow_state.shape, f32),
+        pltpu.VMEM(spacing.shape, f32),
+        pltpu.VMEM(bc_kind.shape, jnp.int32),
+        pltpu.VMEM((1, C), jnp.int32),
+        pltpu.VMEM((1, C), jnp.int32),
+        pltpu.VMEM(abl_temp.shape, f32),
+        pltpu.SMEM(conduct.shape, f32),
+        pltpu.SMEM(conduct.shape, f32),
+        pltpu.SMEM(conduct.shape, f32),
+        dma((chunks,)), dma((8,)),
         pltpu.VMEM((K + 4, 5, I, J), f32),
         pltpu.VMEM((K + 4, 4, I, J), f32),
         pltpu.VMEM((K, 5, 2, J), f32),
@@ -483,20 +553,29 @@
         dma((2,)), dma((2,)), dma((2,)), dma((2,)),
         dma((2, chunks)), dma((2, chunks)),
     ]
-    return pl.pallas_call(
+    hbm = pl.BlockSpec(memory_space=pltpu.HBM)
+    results = pl.pallas_call(
         functools.partial(kernel, dims),
         out_shape=(
             jax.ShapeDtypeStruct(flow_state.shape, f32),
             jax.ShapeDtypeStruct(spacing.shape, f32),
             jax.ShapeDtypeStruct(abl_temp.shape, f32),
         ),
-        in_specs=[vmem] * 6 + [smem] * 3,
-        out_specs=(vmem,) * 3,
+        in_specs=[hbm] * 9,
+        out_specs=(hbm,) * 3,
         scratch_shapes=scratch,
         compiler_params=pltpu.CompilerParams(
-            collective_id=0, has_side_effects=True, vmem_limit_bytes=50 * 1024 * 1024),
+            collective_id=0, has_side_effects=True, vmem_limit_bytes=VMEM_BYTES),
     )(flow_state, spacing, bc_kind, cell_of.reshape(1, C), zone_id.reshape(1, C), abl_temp,
       conduct, diffuse, rate)
+    return pl.pallas_call(
+        hand_out,
+        out_shape=[jax.ShapeDtypeStruct(r.shape, f32) for r in results],
+        in_specs=[hbm] * 3,
+        out_specs=[hbm] * 3,
+        scratch_shapes=[dma((2 + 5 * PIECES,))],
+        compiler_params=pltpu.CompilerParams(vmem_limit_bytes=VMEM_BYTES),
+    )(*results)
 
 
 def solution(mesh):

time: 40.8 us -> 129 us (3.16)
  Pallas kernels: 28.6 us -> 129 us
  local copies, waits for them, and re-layouts: 11.2 us -> 0 us
    pallas_call x0 -> x1, Pallas kernels: none -> 104 us  [shards(): pl.pallas_call(hand_out, out_shape=[jax.ShapeDtypeStruct(r.shape, f32) fo...]
    unnamed x19 -> x0, local copies, waits for them, and re-layouts: 11.2 us -> none
    pallas_call x1, Pallas kernels: 28.6 us -> 24.1 us  [shards(): pl.pallas_call(functools.partial(kernel, dims), out_shape=(jax.ShapeDtype...]
where the time goes in v2:
time: 129 us
  Pallas kernels  129 us (100%)
    pallas_call x1, Pallas kernels, shards(): pl.pallas_call(hand_out, out_shape=[jax.ShapeDtypeStruct(r.shape, f32) fo...  104 us
    pallas_call x1, Pallas kernels, shards(): pl.pallas_call(functools.partial(kernel, dims), out_shape=(jax.ShapeDtype...  24.1 us

profile of v2, /device:TPU:0, one launch (start us, length us, event | category | flops | bytes accessed | tf_op | source)
XLA Modules:
  0.0 129.2 jit_solution(6994757920842253327)
XLA Ops:
  0.6 24.1 %shard_map.112 = (f32[5,32,8,512]{3,2,1,0:T(8,128)}, f32[32,8,512]{2,1,0:T(8,128)}, f32[64,1024]{1,0:T(8,128)}) custom-call(f32[5,32,8,512]{3,2,1,0:T(8,128)} %flow_hbm.1, f32[32,8,512]{2,1,0:T(8,128)} %spacing_hbm.1, s32[8,512]{1,0:T(8,128)} %kind_hbm.1, s32[1,1024]{1,0:T(1,128)} %bitcast.2, s32[1,1024]{1,0:T(1,128)} %bitcast.3, f32[64,1024]{1,0:T(8,128)} %abl_hbm.1, ...), custom_call_target="tpu_custom_call" | custom-call | tf_op jit(solution)/shard_map/pallas_call | solution.py:557
  24.8 104.4 %shard_map.113 = (f32[5,32,8,512]{3,2,1,0:T(8,128)}, f32[32,8,512]{2,1,0:T(8,128)}, f32[64,1024]{1,0:T(8,128)}) custom-call(f32[5,32,8,512]{3,2,1,0:T(8,128)} %get-tuple-element.6.a, f32[32,8,512]{2,1,0:T(8,128)} %get-tuple-element.7.b, f32[64,1024]{1,0:T(8,128)} %get-tuple-element.8.c), custom_call_target="tpu_custom_call" | custom-call | tf_op jit(solution)/shard_map/pallas_call | solution.py:571

commit v3 on v2

--- a/solution.py
+++ b/solution.py
@@ -18,8 +18,12 @@
 far_values = (1.0, 0.5, 0.0, 0.0, 2.625)
 SCALE = time_step / 12.0
 CHUNK = 4
+HAND = 4
 VMEM_BYTES = 62 * 1024 * 1024
-PIECES = 2
+
+
+def bounds_of(K):
+    return (0, 2) + tuple(range(4, K + 1, CHUNK))
 
 
 def parts3(x):
@@ -66,10 +70,10 @@
 def kernel(
     dims,
     flow_hbm, spacing_hbm, kind_hbm, cells_hbm, zones_hbm, abl_hbm, conduct_hbm, diffuse_hbm, rate_hbm,
-    out_hbm, shift_hbm, abl_out_hbm,
+    out_hbm, shift_hbm, abl_out_hbm, RL, RR,
     out, shift_out, abl_out, s_out,
     flow, spacing, kind, cells, zones, abl, conduct, diffuse, rate, s_flow, s_in,
-    F3, Q, XR, XL, RL, RR, PM, V, send_list, recv_list, reply, reply_in,
+    F3, Q, XR, XL, PM, V, send_list, recv_list, reply, reply_in,
     slab_total, totals_in, film_buf, film_in, part, part_in,
     halo_u, halo_s, sp, dense,
     s_list, r_list, s_rep, r_rep, s_tot, r_tot, s_film, r_film, s_part, r_part,
@@ -81,8 +85,11 @@
     s = lax.axis_index("surf")
     w = lax.axis_index("wall")
 
+    cuts = bounds_of(K)
+    chunks = len(cuts) - 1
+
     def flow_copy(c):
-        ks = pl.ds(c * CHUNK, CHUNK)
+        ks = pl.ds(cuts[c], cuts[c + 1] - cuts[c])
         return pltpu.make_async_copy(flow_hbm.at[:, ks], flow.at[:, ks], s_flow.at[c])
 
     pairs = ((spacing_hbm, spacing), (cells_hbm, cells), (zones_hbm, zones), (abl_hbm, abl),
@@ -91,7 +98,7 @@
     flow_copy(0).start()
     for copy in inputs:
         copy.start()
-    for c in range(1, K // CHUNK):
+    for c in range(1, chunks):
         flow_copy(c).start()
     barrier = pltpu.get_barrier_semaphore()
     for d in range(1, NT):
@@ -127,7 +134,7 @@
         )
 
     def side_copies(c):
-        ks = pl.ds(c * CHUNK, CHUNK)
+        ks = pl.ds(cuts[c], cuts[c + 1] - cuts[c])
         return (
             pltpu.make_async_remote_copy(
                 XR.at[ks], RL.at[ks], s_x.at[0, c], r_x.at[0, c],
@@ -190,7 +197,7 @@
 
     def chunk(c, send=True):
         flow_copy(c).wait()
-        lax.fori_loop(c * CHUNK, (c + 1) * CHUNK, surface_terms, 0)
+        lax.fori_loop(cuts[c], cuts[c + 1], surface_terms, 0)
         if send:
             for copy in side_copies(c):
                 copy.start()
@@ -272,7 +279,7 @@
     for d in range(1, NT):
         list_copy(d).start()
 
-    for c in (3, 4, 5):
+    for c in (3, 4, 5, 6):
         chunk(c)
 
     recv_list[0] = send_list[s]
@@ -338,7 +345,7 @@
     for d in range(1, NT):
         reply_copy(d).start()
     reply_in[s] = reply[0]
-    for c in range(6, K // CHUNK):
+    for c in range(7, chunks):
         chunk(c)
 
     for d in range(1, W):
@@ -443,6 +450,8 @@
     lax.fori_loop(0, K, normal_terms, offset)
     shift_copy = pltpu.make_async_copy(shift_out, shift_hbm, s_out.at[0])
     shift_copy.start()
+    out_copy = pltpu.make_async_copy(out, out_hbm, s_out.at[2])
+    out_copy.start()
 
     for d in range(1, NT):
         reply_copy(d).wait()
@@ -465,37 +474,59 @@
     abl_copy = pltpu.make_async_copy(abl_out, abl_out_hbm, s_out.at[1])
     abl_copy.start()
 
+    for c in range(chunks):
+        for copy in side_copies(c):
+            copy.wait()
+    shift_copy.wait()
+    abl_copy.wait()
+    out_copy.wait()
+
+
+def hand_out(
+    state_in, shift_in, abl_in, RL_in, RR_in,
+    state_hbm, shift_hbm, abl_hbm,
+    state, shift, abl, RL, RR, s_in, s_out,
+):
+    K, I = state.shape[1], state.shape[2]
+    size = K // HAND
+
+    def loads(c):
+        ks = pl.ds(c * size, size)
+        return (
+            pltpu.make_async_copy(RL_in.at[ks], RL.at[ks], s_in.at[0, c]),
+            pltpu.make_async_copy(RR_in.at[ks], RR.at[ks], s_in.at[1, c]),
+            pltpu.make_async_copy(state_in.at[:, ks], state.at[:, ks], s_in.at[2, c]),
+        )
+
+    def store(c):
+        ks = pl.ds(c * size, size)
+        return pltpu.make_async_copy(state.at[:, ks], state_hbm.at[:, ks], s_out.at[c])
+
     def add_sides(k, carry):
         for e in range(5):
-            out[e, k, 0:2] = out[e, k, 0:2] + RL[k, e]
-            out[e, k, I - 2 : I] = out[e, k, I - 2 : I] + RR[k, e]
+            state[e, k, 0:2] = state[e, k, 0:2] + RL[k, e]
+            state[e, k, I - 2 : I] = state[e, k, I - 2 : I] + RR[k, e]
         return carry
 
-    def out_copy(c):
-        ks = pl.ds(c * CHUNK, CHUNK)
-        return pltpu.make_async_copy(out.at[:, ks], out_hbm.at[:, ks], s_out.at[2 + c])
-
-    for c in range(K // CHUNK):
-        for copy in side_copies(c):
+    rest = ((shift_in, shift, shift_hbm), (abl_in, abl, abl_hbm))
+    rest_in = [pltpu.make_async_copy(a, b, s_in.at[n, HAND]) for n, (a, b, _) in enumerate(rest)]
+    rest_out = [pltpu.make_async_copy(b, c, s_out.at[HAND + n]) for n, (_, b, c) in enumerate(rest)]
+    for c in range(HAND):
+        for copy in loads(c):
+            copy.start()
+    for copy in rest_in:
+        copy.start()
+    for c in range(HAND):
+        for copy in loads(c):
             copy.wait()
-        lax.fori_loop(c * CHUNK, (c + 1) * CHUNK, add_sides, 0)
-        out_copy(c).start()
-    shift_copy.wait()
-    abl_copy.wait()
-    for c in range(K // CHUNK):
-        out_copy(c).wait()
-
-
-def hand_out(a, b, c, to_a, to_b, to_c, sem):
-    half = a.shape[1] // PIECES
-    copies = [pltpu.make_async_copy(b, to_b, sem.at[0]), pltpu.make_async_copy(c, to_c, sem.at[1])]
-    for e in range(a.shape[0]):
-        for n in range(PIECES):
-            ks = pl.ds(n * half, half)
-            copies.append(pltpu.make_async_copy(a.at[e, ks], to_a.at[e, ks], sem.at[len(copies)]))
-    for copy in copies:
-        copy.start()
-    for copy in copies:
+        lax.fori_loop(c * size, (c + 1) * size, add_sides, 0)
+        store(c).start()
+    for copy, later in zip(rest_in, rest_out):
+        copy.wait()
+        later.start()
+    for c in range(HAND):
+        store(c).wait()
+    for copy in rest_out:
         copy.wait()
 
 
@@ -509,12 +540,12 @@
     count = NT * PT
     dims = (K, I, J, NT, W, C, PT, conduct.shape[0])
     dma = pltpu.SemaphoreType.DMA
-    chunks = K // CHUNK
+    chunks = len(bounds_of(K)) - 1
     scratch = [
         pltpu.VMEM(flow_state.shape, f32),
         pltpu.VMEM(spacing.shape, f32),
         pltpu.VMEM(abl_temp.shape, f32),
-        dma((chunks + 2,)),
+        dma((3,)),
         pltpu.VMEM(flow_state.shape, f32),
         pltpu.VMEM(spacing.shape, f32),
         pltpu.VMEM(bc_kind.shape, jnp.int32),
@@ -527,8 +558,6 @@
         dma((chunks,)), dma((8,)),
         pltpu.VMEM((K + 4, 5, I, J), f32),
         pltpu.VMEM((K + 4, 4, I, J), f32),
-        pltpu.VMEM((K, 5, 2, J), f32),
-        pltpu.VMEM((K, 5, 2, J), f32),
         pltpu.VMEM((K, 5, 2, J), f32),
         pltpu.VMEM((K, 5, 2, J), f32),
         pltpu.VMEM((count, C), bf16),
@@ -560,9 +589,11 @@
             jax.ShapeDtypeStruct(flow_state.shape, f32),
             jax.ShapeDtypeStruct(spacing.shape, f32),
             jax.ShapeDtypeStruct(abl_temp.shape, f32),
+            jax.ShapeDtypeStruct((K, 5, 2, J), f32),
+            jax.ShapeDtypeStruct((K, 5, 2, J), f32),
         ),
         in_specs=[hbm] * 9,
-        out_specs=(hbm,) * 3,
+        out_specs=(hbm,) * 5,
         scratch_shapes=scratch,
         compiler_params=pltpu.CompilerParams(
             collective_id=0, has_side_effects=True, vmem_limit_bytes=VMEM_BYTES),
@@ -570,10 +601,10 @@
       conduct, diffuse, rate)
     return pl.pallas_call(
         hand_out,
-        out_shape=[jax.ShapeDtypeStruct(r.shape, f32) for r in results],
-        in_specs=[hbm] * 3,
+        out_shape=[jax.ShapeDtypeStruct(r.shape, f32) for r in results[:3]],
+        in_specs=[hbm] * 5,
         out_specs=[hbm] * 3,
-        scratch_shapes=[dma((2 + 5 * PIECES,))],
+        scratch_shapes=[pltpu.VMEM(r.shape, f32) for r in results] + [dma((3, HAND + 1)), dma((HAND + 2,))],
         compiler_params=pltpu.CompilerParams(vmem_limit_bytes=VMEM_BYTES),
     )(*results)
 

time: 129 us -> 28 us (0.22)
  Pallas kernels: 129 us -> 27.2 us
    pallas_call x1, Pallas kernels: 104 us -> 3.58 us  [shards(): pl.pallas_call(hand_out, out_shape=[jax.ShapeDtypeStruct(r.shape, f32) fo...]
where the time goes in v3:
time: 28 us; the launch traced here: 27.8 us
  Pallas kernels  27.2 us (97%)
  between operations  0.64 us (2%)
    pallas_call x1, Pallas kernels, shards(): pl.pallas_call(functools.partial(kernel, dims), out_shape=(jax.ShapeDtype...  23.6 us
    pallas_call x1, Pallas kernels, shards(): pl.pallas_call(hand_out, out_shape=[jax.ShapeDtypeStruct(r.shape, f32) fo...  3.58 us

profile of v3, /device:TPU:0, one launch (start us, length us, event | category | flops | bytes accessed | tf_op | source)
XLA Modules:
  0.0 27.8 jit_solution(2734906271787548246)
XLA Ops:
  0.6 23.6 %shard_map.112 = (f32[5,32,8,512]{3,2,1,0:T(8,128)}, f32[32,8,512]{2,1,0:T(8,128)}, f32[64,1024]{1,0:T(8,128)}, f32[32,5,2,512]{3,2,1,0:T(2,128)}, f32[32,5,2,512]{3,2,1,0:T(2,128)}) custom-call(f32[5,32,8,512]{3,2,1,0:T(8,128)} %flow_hbm.1, f32[32,8,512]{2,1,0:T(8,128)} %spacing_hbm.1, s32[8,512]{1,0:T(8,128)} %kind_hbm.1, s32[1,1024]{1,0:T(1,128)} %bitcast.2, ...), custom_call_target="tpu_custom_call" | custom-call | tf_op jit(solution)/shard_map/pallas_call | solution.py:586
  24.2 3.6 %shard_map.113 = (f32[5,32,8,512]{3,2,1,0:T(8,128)}, f32[32,8,512]{2,1,0:T(8,128)}, f32[64,1024]{1,0:T(8,128)}) custom-call(f32[5,32,8,512]{3,2,1,0:T(8,128)} %get-tuple-element.8.state_in, f32[32,8,512]{2,1,0:T(8,128)} %get-tuple-element.9.shift_in, f32[64,1024]{1,0:T(8,128)} %get-tuple-element.10.abl_in, f32[32,5,2,512]{3,2,1,0:T(2,128)} %get-tuple-element.11.RL_in, ...), custom_call_target="tpu_custom_call" | custom-call | tf_op jit(solution)/shard_map/pallas_call | solution.py:602

commit v4 on v3

--- a/solution.py
+++ b/solution.py
@@ -19,7 +19,7 @@
 SCALE = time_step / 12.0
 CHUNK = 4
 HAND = 4
-VMEM_BYTES = 62 * 1024 * 1024
+VMEM_BYTES = 26 * 1024 * 1024
 
 
 def bounds_of(K):
@@ -70,8 +70,7 @@
 def kernel(
     dims,
     flow_hbm, spacing_hbm, kind_hbm, cells_hbm, zones_hbm, abl_hbm, conduct_hbm, diffuse_hbm, rate_hbm,
-    out_hbm, shift_hbm, abl_out_hbm, RL, RR,
-    out, shift_out, abl_out, s_out,
+    out, shift_out, abl_out, RL, RR,
     flow, spacing, kind, cells, zones, abl, conduct, diffuse, rate, s_flow, s_in,
     F3, Q, XR, XL, PM, V, send_list, recv_list, reply, reply_in,
     slab_total, totals_in, film_buf, film_in, part, part_in,
@@ -448,10 +447,6 @@
         return run + here
 
     lax.fori_loop(0, K, normal_terms, offset)
-    shift_copy = pltpu.make_async_copy(shift_out, shift_hbm, s_out.at[0])
-    shift_copy.start()
-    out_copy = pltpu.make_async_copy(out, out_hbm, s_out.at[2])
-    out_copy.start()
 
     for d in range(1, NT):
         reply_copy(d).wait()
@@ -471,32 +466,15 @@
         gain = col_diffuse * (above - 2.0 * profile + below)
         profile = jnp.where(depth_row == 0, profile, profile + gain)
     abl_out[...] = profile
-    abl_copy = pltpu.make_async_copy(abl_out, abl_out_hbm, s_out.at[1])
-    abl_copy.start()
 
     for c in range(chunks):
         for copy in side_copies(c):
             copy.wait()
-    shift_copy.wait()
-    abl_copy.wait()
-    out_copy.wait()
-
-
-def hand_out(
-    state_in, shift_in, abl_in, RL_in, RR_in,
-    state_hbm, shift_hbm, abl_hbm,
-    state, shift, abl, RL, RR, s_in, s_out,
-):
-    K, I = state.shape[1], state.shape[2]
+
+
+def hand_out(state_in, shift, abl, RL, RR, state_hbm, shift_hbm, abl_hbm, state, s_out):
+    K, I, J = state.shape[1:]
     size = K // HAND
-
-    def loads(c):
-        ks = pl.ds(c * size, size)
-        return (
-            pltpu.make_async_copy(RL_in.at[ks], RL.at[ks], s_in.at[0, c]),
-            pltpu.make_async_copy(RR_in.at[ks], RR.at[ks], s_in.at[1, c]),
-            pltpu.make_async_copy(state_in.at[:, ks], state.at[:, ks], s_in.at[2, c]),
-        )
 
     def store(c):
         ks = pl.ds(c * size, size)
@@ -504,29 +482,20 @@
 
     def add_sides(k, carry):
         for e in range(5):
-            state[e, k, 0:2] = state[e, k, 0:2] + RL[k, e]
-            state[e, k, I - 2 : I] = state[e, k, I - 2 : I] + RR[k, e]
+            middle = jnp.zeros((I - 4, J), f32)
+            state[e, k] = state_in[e, k] + jnp.concatenate([RL[k, e], middle, RR[k, e]], axis=0)
         return carry
 
-    rest = ((shift_in, shift, shift_hbm), (abl_in, abl, abl_hbm))
-    rest_in = [pltpu.make_async_copy(a, b, s_in.at[n, HAND]) for n, (a, b, _) in enumerate(rest)]
-    rest_out = [pltpu.make_async_copy(b, c, s_out.at[HAND + n]) for n, (_, b, c) in enumerate(rest)]
-    for c in range(HAND):
-        for copy in loads(c):
-            copy.start()
-    for copy in rest_in:
+    rest = (pltpu.make_async_copy(shift, shift_hbm, s_out.at[HAND]),
+            pltpu.make_async_copy(abl, abl_hbm, s_out.at[HAND + 1]))
+    for copy in rest:
         copy.start()
     for c in range(HAND):
-        for copy in loads(c):
-            copy.wait()
         lax.fori_loop(c * size, (c + 1) * size, add_sides, 0)
         store(c).start()
-    for copy, later in zip(rest_in, rest_out):
-        copy.wait()
-        later.start()
     for c in range(HAND):
         store(c).wait()
-    for copy in rest_out:
+    for copy in rest:
         copy.wait()
 
 
@@ -542,10 +511,6 @@
     dma = pltpu.SemaphoreType.DMA
     chunks = len(bounds_of(K)) - 1
     scratch = [
-        pltpu.VMEM(flow_state.shape, f32),
-        pltpu.VMEM(spacing.shape, f32),
-        pltpu.VMEM(abl_temp.shape, f32),
-        dma((3,)),
         pltpu.VMEM(flow_state.shape, f32),
         pltpu.VMEM(spacing.shape, f32),
         pltpu.VMEM(bc_kind.shape, jnp.int32),
@@ -583,6 +548,10 @@
         dma((2, chunks)), dma((2, chunks)),
     ]
     hbm = pl.BlockSpec(memory_space=pltpu.HBM)
+    vmem = pl.BlockSpec(memory_space=pltpu.VMEM)
+    held = [pltpu.with_memory_space_constraint(x, pltpu.HBM) for x in (
+        flow_state, spacing, bc_kind, cell_of.reshape(1, C), zone_id.reshape(1, C), abl_temp,
+        conduct, diffuse, rate)]
     results = pl.pallas_call(
         functools.partial(kernel, dims),
         out_shape=(
@@ -593,18 +562,17 @@
             jax.ShapeDtypeStruct((K, 5, 2, J), f32),
         ),
         in_specs=[hbm] * 9,
-        out_specs=(hbm,) * 5,
+        out_specs=(vmem,) * 5,
         scratch_shapes=scratch,
         compiler_params=pltpu.CompilerParams(
             collective_id=0, has_side_effects=True, vmem_limit_bytes=VMEM_BYTES),
-    )(flow_state, spacing, bc_kind, cell_of.reshape(1, C), zone_id.reshape(1, C), abl_temp,
-      conduct, diffuse, rate)
+    )(*held)
     return pl.pallas_call(
         hand_out,
         out_shape=[jax.ShapeDtypeStruct(r.shape, f32) for r in results[:3]],
-        in_specs=[hbm] * 5,
+        in_specs=[vmem] * 5,
         out_specs=[hbm] * 3,
-        scratch_shapes=[pltpu.VMEM(r.shape, f32) for r in results] + [dma((3, HAND + 1)), dma((HAND + 2,))],
+        scratch_shapes=[pltpu.VMEM(flow_state.shape, f32), dma((HAND + 2,))],
         compiler_params=pltpu.CompilerParams(vmem_limit_bytes=VMEM_BYTES),
     )(*results)
 

time: 28 us -> 26.1 us (0.932)
  Pallas kernels: 27.2 us -> 25.3 us
    pallas_call x1, Pallas kernels: 3.58 us -> 1.8 us  [shards(): pl.pallas_call(hand_out, out_shape=[jax.ShapeDtypeStruct(r.shape, f32) fo...]
where the time goes in v4:
time: 26.1 us; the launch traced here: 25.9 us
  Pallas kernels  25.3 us (97%)
  between operations  0.64 us (2%)
    pallas_call x1, Pallas kernels, shards(): pl.pallas_call(functools.partial(kernel, dims), out_shape=(jax.ShapeDtype...  23.5 us
    pallas_call x1, Pallas kernels, shards(): pl.pallas_call(hand_out, out_shape=[jax.ShapeDtypeStruct(r.shape, f32) fo...  1.8 us

profile of v4, /device:TPU:0, one launch (start us, length us, event | category | flops | bytes accessed | tf_op | source)
XLA Modules:
  0.0 25.9 jit_solution(16047359371378363359)
XLA Ops:
  0.6 23.5 %shard_map.112 = (f32[5,32,8,512]{3,2,1,0:T(8,128)S(1)}, f32[32,8,512]{2,1,0:T(8,128)S(1)}, f32[64,1024]{1,0:T(8,128)S(1)}, f32[32,5,2,512]{3,2,1,0:T(2,128)S(1)}, f32[32,5,2,512]{3,2,1,0:T(2,128)S(1)}) custom-call(f32[5,32,8,512]{3,2,1,0:T(8,128)} %flow_hbm.1, f32[32,8,512]{2,1,0:T(8,128)} %spacing_hbm.1, s32[8,512]{1,0:T(8,128)} %kind_hbm.1, ...), custom_call_target="tpu_custom_call" | custom-call | tf_op jit(solution)/shard_map/pallas_call | solution.py:555
  24.1 1.8 %shard_map.113 = (f32[5,32,8,512]{3,2,1,0:T(8,128)}, f32[32,8,512]{2,1,0:T(8,128)}, f32[64,1024]{1,0:T(8,128)}) custom-call(f32[5,32,8,512]{3,2,1,0:T(8,128)S(1)} %get-tuple-element.8.state_in, f32[32,8,512]{2,1,0:T(8,128)S(1)} %get-tuple-element.9.shift, f32[64,1024]{1,0:T(8,128)S(1)} %get-tuple-element.10.abl, f32[32,5,2,512]{3,2,1,0:T(2,128)S(1)} %get-tuple-element.11.RL, ...), custom_call_target="tpu_custom_call" | custom-call | tf_op jit(solution)/shard_map/pallas_call | solution.py:570

commit v5 on v4

--- a/solution.py
+++ b/solution.py
@@ -95,15 +95,15 @@
              (kind_hbm, kind), (conduct_hbm, conduct), (diffuse_hbm, diffuse), (rate_hbm, rate))
     inputs = [pltpu.make_async_copy(a, b, s_in.at[n]) for n, (a, b) in enumerate(pairs)]
     flow_copy(0).start()
-    for copy in inputs:
-        copy.start()
-    for c in range(1, chunks):
-        flow_copy(c).start()
     barrier = pltpu.get_barrier_semaphore()
     for d in range(1, NT):
         pl.semaphore_signal(barrier, inc=1, device_id=(lax.rem(s + d, NT), w), device_id_type=MESH)
     for d in range(1, W):
         pl.semaphore_signal(barrier, inc=1, device_id=(s, lax.rem(w + d, W)), device_id_type=MESH)
+    for copy in inputs:
+        copy.start()
+    for c in range(1, chunks):
+        flow_copy(c).start()
 
     def list_copy(d):
         t = lax.rem(s + d, NT)
@@ -236,7 +236,8 @@
         total_copy(d).start()
     totals_in[w] = slab_total[...]
 
-    chunk(2)
+    for c in (2, 3, 4):
+        chunk(c)
 
     for copy in inputs[1:]:
         copy.wait()
@@ -278,7 +279,7 @@
     for d in range(1, NT):
         list_copy(d).start()
 
-    for c in (3, 4, 5, 6):
+    for c in (5, 6):
         chunk(c)
 
     recv_list[0] = send_list[s]

time: 26.1 us -> 27.1 us (1.038)
  Pallas kernels: 25.3 us -> 26.3 us
    pallas_call x1, Pallas kernels: 23.5 us -> 24.5 us  [shards(): pl.pallas_call(functools.partial(kernel, dims), out_shape=(jax.ShapeDtype...]
where the time goes in v5:
time: 27.1 us; the launch traced here: 27 us
  Pallas kernels  26.3 us (97%)
  between operations  0.64 us (2%)
    pallas_call x1, Pallas kernels, shards(): pl.pallas_call(functools.partial(kernel, dims), out_shape=(jax.ShapeDtype...  24.5 us
    pallas_call x1, Pallas kernels, shards(): pl.pallas_call(hand_out, out_shape=[jax.ShapeDtypeStruct(r.shape, f32) fo...  1.8 us

profile of v5, /device:TPU:0, one launch (start us, length us, event | category | flops | bytes accessed | tf_op | source)
XLA Modules:
  0.0 27.0 jit_solution(716736531994913076)
XLA Ops:
  0.6 24.5 %shard_map.112 = (f32[5,32,8,512]{3,2,1,0:T(8,128)S(1)}, f32[32,8,512]{2,1,0:T(8,128)S(1)}, f32[64,1024]{1,0:T(8,128)S(1)}, f32[32,5,2,512]{3,2,1,0:T(2,128)S(1)}, f32[32,5,2,512]{3,2,1,0:T(2,128)S(1)}) custom-call(f32[5,32,8,512]{3,2,1,0:T(8,128)} %flow_hbm.1, f32[32,8,512]{2,1,0:T(8,128)} %spacing_hbm.1, s32[8,512]{1,0:T(8,128)} %kind_hbm.1, ...), custom_call_target="tpu_custom_call" | custom-call | tf_op jit(solution)/shard_map/pallas_call | solution.py:556
  25.1 1.8 %shard_map.113 = (f32[5,32,8,512]{3,2,1,0:T(8,128)}, f32[32,8,512]{2,1,0:T(8,128)}, f32[64,1024]{1,0:T(8,128)}) custom-call(f32[5,32,8,512]{3,2,1,0:T(8,128)S(1)} %get-tuple-element.8.state_in, f32[32,8,512]{2,1,0:T(8,128)S(1)} %get-tuple-element.9.shift, f32[64,1024]{1,0:T(8,128)S(1)} %get-tuple-element.10.abl, f32[32,5,2,512]{3,2,1,0:T(2,128)S(1)} %get-tuple-element.11.RL, ...), custom_call_target="tpu_custom_call" | custom-call | tf_op jit(solution)/shard_map/pallas_call | solution.py:571

commit v6 on v5

--- a/solution.py
+++ b/solution.py
@@ -216,28 +216,7 @@
             copy.start()
 
     chunk(1)
-    inputs[0].wait()
-    def add_total(k, total):
-        layer = spacing[k]
-        sp[k + 2] = layer
-        return total + layer
-
-    slab_total[...] = lax.fori_loop(0, K, add_total, jnp.zeros((I, J), f32))
-    inv, vx, vy, vz, pressure = primitives_of(*[flow[e, 0] for e in range(5)])
-    film_buf[0] = 2.0 / spacing[0]
-    film_buf[1] = pressure * inv + 0.2 * (vx * vx + vy * vy + vz * vz)
-
-    @pl.when(w == 0)
-    def _():
-        for d in range(1, W):
-            film_copy(d).start()
-
-    for d in range(1, W):
-        total_copy(d).start()
-    totals_in[w] = slab_total[...]
-
-    for c in (2, 3, 4):
-        chunk(c)
+    chunk(2)
 
     for copy in inputs[1:]:
         copy.wait()
@@ -279,7 +258,27 @@
     for d in range(1, NT):
         list_copy(d).start()
 
-    for c in (5, 6):
+    inputs[0].wait()
+    def add_total(k, total):
+        layer = spacing[k]
+        sp[k + 2] = layer
+        return total + layer
+
+    slab_total[...] = lax.fori_loop(0, K, add_total, jnp.zeros((I, J), f32))
+    inv, vx, vy, vz, pressure = primitives_of(*[flow[e, 0] for e in range(5)])
+    film_buf[0] = 2.0 / spacing[0]
+    film_buf[1] = pressure * inv + 0.2 * (vx * vx + vy * vy + vz * vz)
+
+    @pl.when(w == 0)
+    def _():
+        for d in range(1, W):
+            film_copy(d).start()
+
+    for d in range(1, W):
+        total_copy(d).start()
+    totals_in[w] = slab_total[...]
+
+    for c in (3, 4, 5):
         chunk(c)
 
     recv_list[0] = send_list[s]
@@ -345,8 +344,27 @@
     for d in range(1, NT):
         reply_copy(d).start()
     reply_in[s] = reply[0]
-    for c in range(7, chunks):
+    for c in range(6, chunks):
         chunk(c)
+
+    for d in range(1, NT):
+        reply_copy(d).wait()
+    answer = jnp.concatenate([reply_in[t, 0:1] for t in range(NT)], axis=1)
+    V[...] = jnp.zeros(V.shape, f32)
+    for n, piece in enumerate(parts3(answer)):
+        V[n : n + 1, 0:count] = piece
+    back = jnp.dot(V[:, 0:count].astype(bf16), PM[...], preferred_element_type=f32)
+    col_surface = back[0:1] + back[1:2] + back[2:3]
+    col_diffuse = pick(zone, diffuse, NZ)
+    depth = abl.shape[0]
+    depth_row = lax.broadcasted_iota(jnp.int32, (depth, C), 0)
+    profile = jnp.where(depth_row == 0, col_surface, abl[...])
+    for heat_pass in range(2):
+        below = pltpu.roll(profile, 1, 0)
+        above = jnp.where(depth_row == depth - 1, below, pltpu.roll(profile, depth - 1, 0))
+        gain = col_diffuse * (above - 2.0 * profile + below)
+        profile = jnp.where(depth_row == 0, profile, profile + gain)
+    abl_out[...] = profile
 
     for d in range(1, W):
         part_copy(d).wait()
@@ -448,25 +466,6 @@
         return run + here
 
     lax.fori_loop(0, K, normal_terms, offset)
-
-    for d in range(1, NT):
-        reply_copy(d).wait()
-    answer = jnp.concatenate([reply_in[t, 0:1] for t in range(NT)], axis=1)
-    V[...] = jnp.zeros(V.shape, f32)
-    for n, piece in enumerate(parts3(answer)):
-        V[n : n + 1, 0:count] = piece
-    back = jnp.dot(V[:, 0:count].astype(bf16), PM[...], preferred_element_type=f32)
-    col_surface = back[0:1] + back[1:2] + back[2:3]
-    col_diffuse = pick(zone, diffuse, NZ)
-    depth = abl.shape[0]
-    depth_row = lax.broadcasted_iota(jnp.int32, (depth, C), 0)
-    profile = jnp.where(depth_row == 0, col_surface, abl[...])
-    for heat_pass in range(2):
-        below = pltpu.roll(profile, 1, 0)
-        above = jnp.where(depth_row == depth - 1, below, pltpu.roll(profile, depth - 1, 0))
-        gain = col_diffuse * (above - 2.0 * profile + below)
-        profile = jnp.where(depth_row == 0, profile, profile + gain)
-    abl_out[...] = profile
 
     for c in range(chunks):
         for copy in side_copies(c):

time: 27.1 us -> 25.8 us (0.952)
  Pallas kernels: 26.3 us -> 25 us
    pallas_call x1, Pallas kernels: 24.5 us -> 23.2 us  [shards(): pl.pallas_call(functools.partial(kernel, dims), out_shape=(jax.ShapeDtype...]
where the time goes in v6:
time: 25.8 us; the launch traced here: 25.7 us
  Pallas kernels  25 us (97%)
  between operations  0.64 us (2%)
    pallas_call x1, Pallas kernels, shards(): pl.pallas_call(functools.partial(kernel, dims), out_shape=(jax.ShapeDtype...  23.2 us
    pallas_call x1, Pallas kernels, shards(): pl.pallas_call(hand_out, out_shape=[jax.ShapeDtypeStruct(r.shape, f32) fo...  1.8 us

profile of v6, /device:TPU:0, one launch (start us, length us, event | category | flops | bytes accessed | tf_op | source)
XLA Modules:
  0.0 25.7 jit_solution(15644585729330994618)
XLA Ops:
  0.6 23.2 %shard_map.112 = (f32[5,32,8,512]{3,2,1,0:T(8,128)S(1)}, f32[32,8,512]{2,1,0:T(8,128)S(1)}, f32[64,1024]{1,0:T(8,128)S(1)}, f32[32,5,2,512]{3,2,1,0:T(2,128)S(1)}, f32[32,5,2,512]{3,2,1,0:T(2,128)S(1)}) custom-call(f32[5,32,8,512]{3,2,1,0:T(8,128)} %flow_hbm.1, f32[32,8,512]{2,1,0:T(8,128)} %spacing_hbm.1, s32[8,512]{1,0:T(8,128)} %kind_hbm.1, ...), custom_call_target="tpu_custom_call" | custom-call | tf_op jit(solution)/shard_map/pallas_call | solution.py:555
  23.9 1.8 %shard_map.113 = (f32[5,32,8,512]{3,2,1,0:T(8,128)}, f32[32,8,512]{2,1,0:T(8,128)}, f32[64,1024]{1,0:T(8,128)}) custom-call(f32[5,32,8,512]{3,2,1,0:T(8,128)S(1)} %get-tuple-element.8.state_in, f32[32,8,512]{2,1,0:T(8,128)S(1)} %get-tuple-element.9.shift, f32[64,1024]{1,0:T(8,128)S(1)} %get-tuple-element.10.abl, f32[32,5,2,512]{3,2,1,0:T(2,128)S(1)} %get-tuple-element.11.RL, ...), custom_call_target="tpu_custom_call" | custom-call | tf_op jit(solution)/shard_map/pallas_call | solution.py:570

commit v7 on v6

--- a/solution.py
+++ b/solution.py
@@ -216,7 +216,6 @@
             copy.start()
 
     chunk(1)
-    chunk(2)
 
     for copy in inputs[1:]:
         copy.wait()
@@ -278,7 +277,7 @@
         total_copy(d).start()
     totals_in[w] = slab_total[...]
 
-    for c in (3, 4, 5):
+    for c in (2, 3, 4, 5):
         chunk(c)
 
     recv_list[0] = send_list[s]

time: 25.8 us -> 26.3 us (1.019)
  Pallas kernels: 25 us -> 25.5 us
    pallas_call x1, Pallas kernels: 23.2 us -> 23.7 us  [shards(): pl.pallas_call(functools.partial(kernel, dims), out_shape=(jax.ShapeDtype...]
where the time goes in v7:
time: 26.3 us; the launch traced here: 26.2 us
  Pallas kernels  25.5 us (97%)
  between operations  0.64 us (2%)
    pallas_call x1, Pallas kernels, shards(): pl.pallas_call(functools.partial(kernel, dims), out_shape=(jax.ShapeDtype...  23.7 us
    pallas_call x1, Pallas kernels, shards(): pl.pallas_call(hand_out, out_shape=[jax.ShapeDtypeStruct(r.shape, f32) fo...  1.8 us

profile of v7, /device:TPU:0, one launch (start us, length us, event | category | flops | bytes accessed | tf_op | source)
XLA Modules:
  0.0 26.2 jit_solution(17919931439850123214)
XLA Ops:
  0.6 23.7 %shard_map.112 = (f32[5,32,8,512]{3,2,1,0:T(8,128)S(1)}, f32[32,8,512]{2,1,0:T(8,128)S(1)}, f32[64,1024]{1,0:T(8,128)S(1)}, f32[32,5,2,512]{3,2,1,0:T(2,128)S(1)}, f32[32,5,2,512]{3,2,1,0:T(2,128)S(1)}) custom-call(f32[5,32,8,512]{3,2,1,0:T(8,128)} %flow_hbm.1, f32[32,8,512]{2,1,0:T(8,128)} %spacing_hbm.1, s32[8,512]{1,0:T(8,128)} %kind_hbm.1, ...), custom_call_target="tpu_custom_call" | custom-call | tf_op jit(solution)/shard_map/pallas_call | solution.py:554
  24.4 1.8 %shard_map.113 = (f32[5,32,8,512]{3,2,1,0:T(8,128)}, f32[32,8,512]{2,1,0:T(8,128)}, f32[64,1024]{1,0:T(8,128)}) custom-call(f32[5,32,8,512]{3,2,1,0:T(8,128)S(1)} %get-tuple-element.8.state_in, f32[32,8,512]{2,1,0:T(8,128)S(1)} %get-tuple-element.9.shift, f32[64,1024]{1,0:T(8,128)S(1)} %get-tuple-element.10.abl, f32[32,5,2,512]{3,2,1,0:T(2,128)S(1)} %get-tuple-element.11.RL, ...), custom_call_target="tpu_custom_call" | custom-call | tf_op jit(solution)/shard_map/pallas_call | solution.py:569
